TPU v7x, 512 devices: a whole 4x8x8 slice. The times are simulated.
512 devices in a mesh: replica: 32 (over z, x), tensor: 16 (over y, core).
Axes of the slice: x: 4, y: 8, z: 8, core: 2. Of those that a mesh axis runs over, the one named last changes fastest.
Arguments:
- queries: bfloat16 [4, 128, 8192], P(None, 'replica'), may hold values from -16 to 16
- new_entries: bfloat16 [4, 128, 8, 256], P(None, 'replica'), may hold values from -6 to 6
- cache: bfloat16 [128, 8, 512, 256], P('replica', None, 'tensor'), may hold values from -6 to 6
- lengths: int32 [128], P('replica'), may hold values from 2 to 512
- adapter_pages: bfloat16 [256, 2, 64, 8192], P('replica', None, None, 'tensor'), may hold values from -0.75 to 0.75
- request_slots: int32 [128], P('replica'), may hold values from 0 to 39
- source_replica: int32 [1024, 1], P('replica'), may hold values from 0 to 31; in each aligned block of 32 rows (0 to 31, 32 to 63, ...) at most 2 rows name the same one
- source_slot: int32 [1024], P('replica'), may hold values from 0 to 7
Outputs:
- attended: bfloat16 [4, 128, 8192], P(None, 'replica', 'tensor')
- adapted: bfloat16 [4, 128, 8192], P(None, 'replica', 'tensor')
Inputs may be any that keep to these rules, and one draw needn't show every extreme that they name: `source_replica`: within the 32 plan entries of one replica no source replica appears more than 2 times, and some replica's plan names one source exactly 2 times.
All inputs are finite; a program needn't handle non-finite values.
Results may differ from a plain program's by a relative error of at most 0.019.
Values may be sent and summed in bfloat16 or wider, within the bound.
No kernel may reach another device: no remote copies, remote signals or barrier semaphores. Data moves between devices by JAX's collectives and lax.ppermute only.
A program may use at most 128 MiB of HBM per device.

v0:
```python
import jax
import jax.numpy as jnp
from jax import lax
from jax.sharding import PartitionSpec as P

CAP = 2


neg_large = -1e30
adapter_scale = 0.5


def joined(array, axis, combine):
    everything = jax.tree.map(lambda part: lax.all_gather(part, axis), array)
    initial = jax.tree.map(lambda part: part[0], everything)

    def turn(k, so_far):
        return combine(so_far, jax.tree.map(lambda part: part[k], everything))

    return lax.fori_loop(1, lax.axis_size(axis), turn, initial)


def joint(first, second):
    first_running_maximum, total_first, accum_first = first
    top_second, total_second, accum_second = second
    larger = jnp.maximum(first_running_maximum, top_second)
    fade_first = jnp.exp(first_running_maximum - larger)
    fade_second = jnp.exp(top_second - larger)
    spread = accum_first.shape[-1] // first_running_maximum.shape[-1]
    merged_accum = accum_first * jnp.repeat(
        fade_first, spread, axis=-1
    ) + accum_second * jnp.repeat(fade_second, spread, axis=-1)
    return (larger, total_first * fade_first + total_second * fade_second, merged_accum)


def per_device(
    queries, new_entries, cache, lengths, adapter_pages, request_slots, source_replica, source_slot
):
    replica_count = lax.axis_size("replica")
    replica_here = lax.axis_index("replica")
    tensor_count = lax.axis_size("tensor")
    tensor_here = lax.axis_index("tensor")
    step_count, row_count, model_width = queries.shape
    kv_count = new_entries.shape[2]
    head_size = new_entries.shape[3] // 2
    head_count = model_width // head_size
    query_group_width = head_count // kv_count
    local_length = cache.shape[2]
    move_count = source_slot.shape[0]
    shard_width = model_width // tensor_count
    page_shape = adapter_pages.shape[1:]
    grouped = queries.reshape(step_count, row_count, kv_count, query_group_width, head_size)
    key_part = cache[..., :head_size]
    value_part = cache[..., head_size:]
    new_keys = new_entries[..., :head_size]
    new_values = new_entries[..., head_size:]
    factor = head_size ** (-0.5)
    cache_scores = (
        jnp.einsum("srkgd,rkld->srkgl", grouped, key_part, preferred_element_type=jnp.float32)
        * factor
    )
    positions = tensor_here * local_length + jnp.arange(local_length, dtype=jnp.int32)
    visible = (positions[None, :] < lengths[:, None])[None, :, None, None, :]
    cache_scores = jnp.where(visible, cache_scores, neg_large)
    fresh_scores = (
        jnp.einsum("srkgd,jrkd->srkgj", grouped, new_keys, preferred_element_type=jnp.float32)
        * factor
    )
    step_ids = jnp.arange(step_count, dtype=jnp.int32)
    causal = (step_ids[:, None] >= step_ids[None, :])[:, None, None, None, :] & (tensor_here == 0)
    fresh_scores = jnp.where(causal, fresh_scores, neg_large)
    top = jnp.maximum(jnp.max(cache_scores, axis=-1), jnp.max(fresh_scores, axis=-1))
    cache_weights = jnp.where(visible, jnp.exp(cache_scores - top[..., None]), 0.0)
    fresh_weights = jnp.where(causal, jnp.exp(fresh_scores - top[..., None]), 0.0)
    total = jnp.sum(cache_weights, axis=-1) + jnp.sum(fresh_weights, axis=-1)
    accum = jnp.einsum(
        "srkgl,rkld->srkgd",
        cache_weights.astype(jnp.bfloat16),
        value_part,
        preferred_element_type=jnp.float32,
    )
    accum = accum + jnp.einsum(
        "srkgj,jrkd->srkgd",
        fresh_weights.astype(jnp.bfloat16),
        new_values,
        preferred_element_type=jnp.float32,
    )
    top = top.reshape(step_count, row_count, head_count)
    total = total.reshape(step_count, row_count, head_count)
    accum = accum.reshape(step_count, row_count, model_width)
    merged_top, merged_total, merged_accum = joined((top, total, accum), "tensor", joint)
    own_accum = lax.dynamic_slice_in_dim(merged_accum, tensor_here * shard_width, shard_width, 2)
    own_total = lax.dynamic_slice_in_dim(
        jnp.repeat(merged_total, head_size, axis=-1), tensor_here * shard_width, shard_width, 2
    )
    attended = (own_accum / own_total).astype(jnp.bfloat16)
    own_sources = source_replica[:, 0]
    all_sources, all_slots = (
        lax.all_gather(own_sources, "replica", axis=0, tiled=True),
        lax.all_gather(source_slot, "replica", axis=0, tiled=True),
    )
    mine = (all_sources == replica_here).astype(jnp.int32).reshape(replica_count, move_count)
    before = jnp.cumsum(mine, axis=1) - mine
    places = jnp.arange(CAP, dtype=jnp.int32)
    picked = (mine[:, None, :] == 1) & (before[:, None, :] == places[None, :, None])
    send_slots = jnp.sum(
        jnp.where(picked, all_slots.reshape(replica_count, 1, move_count), 0), axis=2
    )
    outgoing = jnp.take(adapter_pages, send_slots.reshape(-1), axis=0).reshape(
        (replica_count, CAP) + page_shape
    )
    incoming_rows_here = lax.all_to_all(
        outgoing, "replica", split_axis=0, concat_axis=0, tiled=True
    )
    entry_ids = jnp.arange(move_count, dtype=jnp.int32)
    earlier = (own_sources[:, None] == own_sources[None, :]) & (
        entry_ids[:, None] > entry_ids[None, :]
    )
    rank_within = jnp.sum(earlier.astype(jnp.int32), axis=1)
    flat_arrived = incoming_rows_here.reshape((replica_count * CAP,) + page_shape)
    inbox = jnp.take(flat_arrived, own_sources * CAP + rank_within, axis=0)
    table = jnp.concatenate([adapter_pages, inbox], axis=0)
    expand_rows = jnp.take(table[:, 1], request_slots, axis=0)
    shrink_rows = jnp.take(table[:, 0], request_slots, axis=0)
    shrink_part = jnp.einsum(
        "srd,rkd->srk", attended, shrink_rows, preferred_element_type=jnp.float32
    )
    down_projection = lax.psum(shrink_part, "tensor").astype(jnp.bfloat16)
    adapted = (
        jnp.einsum("vew,ewl->vel", down_projection, expand_rows, preferred_element_type=jnp.float32)
        * adapter_scale
    )
    return (attended, adapted.astype(jnp.bfloat16))


def solution(mesh):
    return jax.shard_map(
        per_device,
        mesh=mesh,
        in_specs=(
            P(None, "replica", None),
            P(None, "replica", None, None),
            P("replica", None, "tensor", None),
            P("replica"),
            P("replica", None, None, "tensor"),
            P("replica"),
            P("replica", None),
            P("replica"),
        ),
        out_specs=(P(None, "replica", "tensor"), P(None, "replica", "tensor")),
        check_vma=False,
    )
```

profile of v0, /device:TPU:1, one launch (start us, length us, event | category | flops | bytes accessed | tf_op | source)
XLA Modules:
  0.0 294.4 jit_solution(10763888366080179598)
XLA Ops:
  7.2 1.2 reshape.192
  8.5 0.8 fusion.50
  9.3 0.7 broadcast_compare_fusion.1
  10.0 1.3 fusion.52
  11.3 1.3 fusion.51
  12.7 1.3 fusion.15
  13.9 0.4 fusion.6
  14.3 1.1 all_gather_reshape.2
  15.4 1.3 dynamic-slice
  17.4 0.2 dynamic-update-slice.1
  17.7 23.1 %all-reduce.2 = (s32[1024]{0:T(1024)S(1)}, s32[1024]{0:T(1024)S(1)}) all-reduce(s32[1024]{0:T(1024)S(1)} %dynamic-update-slice.1, s32[1024]{0:T(1024)S(1)} %bitcast_dynamic-update-slice_fusion), channel_id=1, replica_groups=mesh['replica'=32,'tensor'=16] {'replica'}, use_global_device_ids=true, to_apply=%add.1 | all-reduce | flops 2048 | bytes 16384
  41.7 5.5 %gather_fusion = bf16[64,2,64,512]{3,2,1,0:T(8,128)(2,1)} fusion(bf16[8,2,64,512]{3,2,1,0:T(8,128)(2,1)S(1)} %copy-done, s32[1024]{0:T(1024)S(1)} %pad_clamp_fusion.2), kind=kCustom, calls=%fused_computation.2 | custom fusion | bytes 16777472 | tf_op jit(solution)/shard_map/jit(_take)/gather | solution.py:109
  47.2 7.6 %broadcast_select_fusion = bf16[32,2,2,64,512]{4,3,2,1,0:T(8,128)(2,1)} fusion(bf16[32,2,2,64,512]{4,3,2,1,0:T(8,128)(2,1)} %bitcast.93, pred[32,2]{1,0:T(8,128)(4,1)S(1)} %copy.47), kind=kLoop, calls=%fused_computation.12 | loop fusion | flops 4194304 | bytes 16777280 | tf_op jit(solution)/shard_map/jit(_take)/select_n | solution.py:109
  54.8 5.1 %all-to-all-start = ((bf16[32,2,2,64,512]{4,3,2,1,0:T(8,128)(2,1)}), bf16[32,2,2,64,512]{4,3,2,1,0:T(8,128)(2,1)}, u32[]{:S(2)}, u32[]{:S(2)}) async-start(bf16[32,2,2,64,512]{4,3,2,1,0:T(8,128)(2,1)} %broadcast_select_fusion), calls=%async_computation | async-start | bytes 16777216 | tf_op jit(solution)/shard_map/all_to_all | solution.py:112
  59.9 0.3 fusion.31
  60.2 0.4 fusion.14
  60.9 23.1 %all_gather.16 = f32[16,4,4,64]{3,2,1,0:T(4,128)S(1)} all-gather(f32[1,4,4,64]{3,2,1,0:T(4,128)S(1)} %add.133), channel_id=1, replica_groups=mesh['replica'=32,'tensor'=16] {'tensor'}, dimensions={0}, use_global_device_ids=true | all-gather | bytes 69632 | tf_op jit(solution)/shard_map/all_gather | solution.py:14
  84.0 15.4 %all_gather.15 = f32[16,4,4,64]{3,2,1,0:T(4,128)S(1)} all-gather(f32[1,4,4,64]{3,2,1,0:T(4,128)S(1)} %max.28), channel_id=1, replica_groups=mesh['replica'=32,'tensor'=16] {'tensor'}, dimensions={0}, use_global_device_ids=true | all-gather | bytes 69632 | tf_op jit(solution)/shard_map/all_gather | solution.py:14
  99.8 1.1 slice_bitcast_fusion
  100.8 32.8 %while.19 = (s32[]{:T(128)}, f32[4,4,64]{2,1,0:T(4,128)S(1)}, f32[4,4,64]{2,1,0:T(4,128)S(1)}, f32[4,4,8192]{2,1,0:T(4,128)S(1)}, f32[16,4,4,64]{3,2,1,0:T(4,128...) while((s32[]{:T(128)}, f32[4,4,64]{2,1,0:T(4,128)S(1)}, ...), condition=%wide.region_5.6_spmd, body=%wide.region_4.5_spmd.sunk | while | flops 399365 | bytes 5808279 | solution.py:20
  101.7 1.3 fusion.57
  103.7 0.2 reshape.261
  103.9 1.3 fusion.57
  105.9 0.2 reshape.261
  106.1 1.3 fusion.57
  108.1 0.2 reshape.261
  108.3 1.3 fusion.57
  110.5 1.3 fusion.57
  112.6 1.3 fusion.57
  114.8 1.3 fusion.57
  117.0 1.3 fusion.57
  119.2 1.3 fusion.57
  121.4 1.3 fusion.57
  123.6 1.3 fusion.57
  125.8 1.3 fusion.57
  128.0 1.3 fusion.57
  130.1 1.3 fusion.57
  132.3 1.3 fusion.57
  134.1 105.9 %all-to-all-done = bf16[32,2,2,64,512]{4,3,2,1,0:T(8,128)(2,1)} async-done(((bf16[32,2,2,64,512]{4,3,2,1,0:T(8,128)(2,1)}), bf16[32,2,2,64,512]{4,3,2,1,0:T(8,128)(2,1)}, u32[]{:S(2)}, u32[]{:S(2)}) %all-to-all-start) | async-done | bytes 8388640 | tf_op jit(solution)/shard_map/all_to_all | solution.py:112
  240.0 6.1 %gather_fusion.1 = bf16[32,2,64,512]{3,2,1,0:T(8,128)(2,1)} fusion(bf16[64,2,64,512]{3,2,1,0:T(8,128)(2,1)} %bitcast.23, s32[1024]{0:T(1024)S(1)} %pad_clamp_fusion.1), kind=kCustom, calls=%fused_computation.3 | custom fusion | bytes 8388736 | tf_op jit(solution)/shard_map/jit(_take)/gather | solution.py:121
  246.1 2.6 broadcast_select_fusion.1
  248.8 2.6 fusion.5
  251.4 2.3 gather_fusion.3
  253.7 0.2 convolution_bitcast_fusion
  253.9 30.5 %psum.7 = bf16[4,4,64]{2,0,1:T(4,128)(2,1)S(1)} all-reduce(f32[4,4,64]{2,0,1:T(4,128)S(1)} %convolution_bitcast_fusion), channel_id=1, replica_groups=mesh['replica'=32,'tensor'=16] {'tensor'}, use_global_device_ids=true, to_apply=%region_9.11 | all-reduce | flops 1024 | bytes 6144 | tf_op jit(solution)/shard_map/psum | solution.py:128
  284.4 2.3 gather_fusion.2
  286.7 0.2 fusion.12
  287.0 0.6 copy.50
  (121 shorter events, 13.6 us)
Async XLA Ops:
  7.2 92.6 %all-gather.3.cloned.1.call-start = ((), (), s32[]{:S(2)}) async-start(), calls=%async_computation.1 | async-start | bytes 8912896 | tf_op jit(solution)/shard_map/all_gather | solution.py:14
  8.5 8.9 %copy-start.3 = (s32[32]{0:T(128)S(1)}, s32[32]{0:T(128)}, u32[]{:S(2)}) copy-start(s32[32]{0:T(128)} %param.19) | copy-start | bytes 388
  8.5 9.2 %copy-start.2 = (s32[32,1]{0,1:T(1,128)S(1)}, s32[32,1]{0,1:T(1,128)}, u32[]{:S(2)}) copy-start(s32[32,1]{0,1:T(1,128)} %param.18) | copy-start | bytes 388
  10.0 31.7 %copy-start = (bf16[8,2,64,512]{3,2,1,0:T(8,128)(2,1)S(1)}, bf16[8,2,64,512]{3,2,1,0:T(8,128)(2,1)}, u32[]{:S(2)}) copy-start(bf16[8,2,64,512]{3,2,1,0:T(8,128)(2,1)} %param.16) | copy-start | bytes 3145732
  54.8 44.8 %copy-start.4 = (s32[4]{0:T(128)S(1)}, s32[4]{0:T(128)}, u32[]{:S(2)}) copy-start(s32[4]{0:T(128)} %param.17) | copy-start | bytes 52
  54.8 185.2 %all-to-all-start = ((bf16[32,2,2,64,512]{4,3,2,1,0:T(8,128)(2,1)}), bf16[32,2,2,64,512]{4,3,2,1,0:T(8,128)(2,1)}, u32[]{:S(2)}, u32[]{:S(2)}) async-start(bf16[32,2,2,64,512]{4,3,2,1,0:T(8,128)(2,1)} %broadcast_select_fusion), calls=%async_computation | async-start | bytes 16777216 | tf_op jit(solution)/shard_map/all_to_all | solution.py:112
  134.1 119.6 %copy-start.1 = (bf16[4,4,512]{2,1,0:T(4,128)(2,1)}, bf16[4,4,512]{2,1,0:T(4,128)(2,1)S(1)}, u32[]{:S(2)}) copy-start(bf16[4,4,512]{2,1,0:T(4,128)(2,1)S(1)} %fusion.38) | copy-start | bytes 49156
Sparse Core Ops, SparseCore 0:
  15.5 64.5 all-gather.2
where the time goes:
time: 296 us; the launch traced here: 294 us
  waiting for transfers between devices  106 us (36%)
  blocking collectives  92.2 us (31%)
  local copies, waits for them, and re-layouts  35.6 us (12%)
  other arithmetic  35.1 us (12%)
  between operations  15 us (5%)
  starting transfers between devices  5.15 us (2%)
  matrix products  4.69 us (2%)
    all_to_all x1, waiting for transfers between devices, per_device(): lax.all_to_all(outgoing, 'replica', split_axis=0, concat_axis=0, tiled=True)  106 us
    all_gather x2, blocking collectives, joined(): everything = jax.tree.map(lambda part: lax.all_gather(part, axis), array)  38.6 us
    psum x1, blocking collectives, per_device(): down_projection = lax.psum(shrink_part, 'tensor').astype(jnp.bfloat16)  30.5 us
    unnamed x1, blocking collectives  23.1 us
    add x15, other arithmetic, joint(): accum_first * jnp.repeat(fade_first, spread, axis=-1)  19.6 us
    select_n x2, other arithmetic, per_device(): jnp.take(adapter_pages, send_slots.reshape(-1), axis=0)  7.63 us
    gather x1, local copies, waits for them, and re-layouts, per_device(): inbox = jnp.take(flat_arrived, own_sources * CAP + rank_within, axis=0)  6.12 us
  transfers between devices with their start and end apart: 2, of which 1 were waited for; matrix products, arithmetic and copies ran while one was open for 17% of the time, Pallas kernels for 0%

commit v1 on v0

v1 whole, which is shorter than its diff:
```python
import jax
import jax.numpy as jnp
from jax import lax
from jax.experimental import pallas as pl
from jax.experimental.pallas import tpu as pltpu
from jax.sharding import PartitionSpec as P

f32 = jnp.float32
bf16 = jnp.bfloat16

X_SIZE = 4
SLOTS = 8
ADAPTER_SCALE = 0.5
NEG_LARGE = -1e30
LANES = 128


def vmem_spec():
    return pl.BlockSpec(memory_space=pltpu.VMEM)


def smem_spec():
    return pl.BlockSpec(memory_space=pltpu.SMEM)


def params():
    return pltpu.CompilerParams(vmem_limit_bytes=32 * 1024 * 1024)


def iota(shape, axis):
    return lax.broadcasted_iota(jnp.int32, shape, axis)


def attention_kernel(lengths_ref, q_ref, new_ref, cache_ref, out_ref, q_rows):
    steps, rows, width = q_ref.shape
    kv_heads, local = cache_ref.shape[1], cache_ref.shape[2]
    head = cache_ref.shape[3] // 2
    group = width // head // kv_heads
    tensor_here = lax.axis_index("tensor")
    sr = steps * rows
    count = group * sr
    for s in range(steps):
        q_rows[s * rows : (s + 1) * rows, :] = q_ref[s].astype(f32)
    new_all = new_ref[...].astype(f32).reshape(steps * rows * kv_heads, 2 * head).astype(bf16)
    new_keys, new_values = new_all[:, :head], new_all[:, head:]
    shape = (count, rows * local)
    row_id, col_id = iota(shape, 0), iota(shape, 1)
    request, step = row_id % rows, (row_id // rows) % steps
    col_request = col_id // local
    length = jnp.zeros(shape, jnp.int32)
    for r in range(rows):
        length = jnp.where(col_request == r, lengths_ref[r], length)
    visible = (request == col_request) & (tensor_here * local + col_id % local < length)
    fresh_shape = (count, steps * rows * kv_heads)
    fresh_col = iota(fresh_shape, 1)
    fresh_row = iota(fresh_shape, 0)
    fresh = (
        (fresh_row % rows == (fresh_col // kv_heads) % rows)
        & (fresh_col // (kv_heads * rows) <= (fresh_row // rows) % steps)
        & (tensor_here == 0)
    )
    fresh_head = fresh_col % kv_heads
    factor = head ** (-0.5)
    contract = (((1,), (1,)), ((), ()))
    lane = iota((sr, LANES), 1)
    per_tile = out_ref.shape[2] // head - 1
    for g in range(kv_heads):
        q = jnp.concatenate(
            [q_rows[:, (g * group + k) * head : (g * group + k + 1) * head] for k in range(group)],
            axis=0,
        ).astype(bf16)
        keys = cache_ref[:, g, :, :head].reshape(rows * local, head)
        values = cache_ref[:, g, :, head:].reshape(rows * local, head)
        fresh_here = fresh & (fresh_head == g)
        old_scores = lax.dot_general(q, keys, contract, preferred_element_type=f32) * factor
        new_scores = lax.dot_general(q, new_keys, contract, preferred_element_type=f32) * factor
        old_scores = jnp.where(visible, old_scores, NEG_LARGE)
        new_scores = jnp.where(fresh_here, new_scores, NEG_LARGE)
        top = jnp.max(jnp.maximum(old_scores, new_scores), axis=1, keepdims=True)
        shift = top.astype(bf16).astype(f32)
        old_weights = jnp.where(visible, jnp.exp(old_scores - shift), 0.0)
        new_weights = jnp.where(fresh_here, jnp.exp(new_scores - shift), 0.0)
        total = jnp.sum(old_weights + new_weights, axis=1, keepdims=True)
        accum = jnp.dot(old_weights.astype(bf16), values, preferred_element_type=f32)
        accum = accum + jnp.dot(new_weights.astype(bf16), new_values, preferred_element_type=f32)
        high = total.astype(bf16).astype(f32)
        low = total - high
        for first in range(0, group, per_tile):
            place = (g * group + first) // per_tile
            stats = jnp.zeros((sr, LANES), f32)
            for k in range(per_tile):
                part = slice((first + k) * sr, (first + k + 1) * sr)
                out_ref[place, :, k * head : (k + 1) * head] = accum[part].astype(bf16)
                stats = jnp.where(lane == k, shift[part], stats)
                stats = jnp.where(lane == per_tile + k, high[part], stats)
                stats = jnp.where(lane == 2 * per_tile + k, low[part], stats)
            out_ref[place, :, per_tile * head :] = stats.astype(bf16)


def combine_kernel(slots_ref, source_ref, source_slot_ref, part_ref, attended_ref, send_ref):
    steps, rows, width = attended_ref.shape
    sources = part_ref.shape[0]
    per_tile = width // LANES
    stats = [part_ref[t, :, width:].astype(f32) for t in range(sources)]
    top = stats[0]
    for t in range(1, sources):
        top = jnp.maximum(top, stats[t])
    sums = [jnp.zeros((steps * rows, LANES), f32) for _ in range(per_tile)]
    total = jnp.zeros((steps * rows, LANES), f32)
    for t in range(sources):
        fade = jnp.exp(stats[t] - top)
        both = pltpu.roll(stats[t], LANES - per_tile, 1) + pltpu.roll(
            stats[t], LANES - 2 * per_tile, 1
        )
        total = total + fade * both
        for k in range(per_tile):
            sums[k] = sums[k] + fade[:, k : k + 1] * part_ref[
                t, :, k * LANES : (k + 1) * LANES
            ].astype(f32)
    replica_here = lax.axis_index("replica")
    row = iota((steps * rows, LANES), 0) % rows
    page = jnp.zeros((steps * rows, LANES), f32)
    for r in range(rows):
        slot = slots_ref[r]
        entry = jnp.clip(slot - SLOTS, 0, source_slot_ref.shape[0] - 1)
        number = jnp.where(
            slot < SLOTS,
            replica_here * SLOTS + slot,
            source_ref[entry] * SLOTS + source_slot_ref[entry],
        )
        page = jnp.where(row == r, number.astype(f32), page)
    page = page.astype(bf16)
    for k in range(per_tile):
        attended = sums[k] / total[:, k : k + 1]
        for s in range(steps):
            attended_ref[s, :, k * LANES : (k + 1) * LANES] = attended[
                s * rows : (s + 1) * rows
            ].astype(bf16)
        rounded = attended.astype(bf16)
        for z in range(send_ref.shape[0]):
            send_ref[z, :, k * LANES : (k + 1) * LANES] = rounded
    for z in range(send_ref.shape[0]):
        send_ref[z, :, width:] = page


def page_columns(page, first, rank, width):
    return page[:, :1] == (first + iota((page.shape[0], width), 1) // rank).astype(f32)


def shrink_kernel(rows_ref, shrink_ref, out_ref):
    z_count, rows, padded = rows_ref.shape
    pages, rank, width = shrink_ref.shape
    count = z_count * rows
    at_once = 256 // rank
    data = rows_ref[...].reshape(count, padded)
    x, page = data[:, :width], data[:, width:].astype(f32)
    base = lax.axis_index("replica") // X_SIZE * (X_SIZE * SLOTS)
    accum = jnp.zeros((count, at_once * rank), f32)
    for p in range(0, pages, at_once):
        block = shrink_ref[p : p + at_once].reshape(at_once * rank, width)
        product = lax.dot_general(x, block, (((1,), (1,)), ((), ())), preferred_element_type=f32)
        accum = accum + jnp.where(
            page_columns(page, base + p, rank, at_once * rank), product, 0.0
        )
    folded = accum[:, :LANES] + accum[:, LANES:]
    folded = folded + pltpu.roll(folded, rank, 1)
    half = count // 2
    packed = jnp.where(iota((half, LANES), 1) < rank, folded[:half], folded[half:]).astype(bf16)
    for t in range(out_ref.shape[0]):
        out_ref[t] = packed


def expand_kernel(part_ref, rows_ref, expand_ref, out_ref):
    z_count, rows, padded = rows_ref.shape
    pages, rank, width = expand_ref.shape
    count = z_count * rows
    at_once = 256 // rank
    page = rows_ref[:, :, width:].reshape(count, padded - width).astype(f32)
    base = lax.axis_index("replica") // X_SIZE * (X_SIZE * SLOTS)
    packed = part_ref[0].astype(f32)
    for t in range(1, part_ref.shape[0]):
        packed = packed + part_ref[t].astype(f32)
    swapped = pltpu.roll(packed, rank, 1)
    left = iota(packed.shape, 1) < rank
    low = jnp.concatenate(
        [jnp.where(left, packed, swapped), jnp.where(left, swapped, packed)], axis=0
    )
    low = jnp.concatenate([low, low], axis=1).astype(bf16).astype(f32)
    accum = jnp.zeros((count, width), f32)
    for p in range(0, pages, at_once):
        block = expand_ref[p : p + at_once].reshape(at_once * rank, width)
        used = jnp.where(page_columns(page, base + p, rank, at_once * rank), low, 0.0)
        accum = accum + jnp.dot(used.astype(bf16), block, preferred_element_type=f32)
    out_ref[...] = (accum * ADAPTER_SCALE).astype(bf16).reshape(z_count, rows, width)


def gather_kernel(part_ref, out_ref):
    steps, rows, _ = out_ref.shape
    total = part_ref[0].astype(f32)
    for z in range(1, part_ref.shape[0]):
        total = total + part_ref[z].astype(f32)
    for s in range(steps):
        out_ref[s] = total[s * rows : (s + 1) * rows].astype(bf16)


def per_device(
    queries, new_entries, cache, lengths, adapter_pages, request_slots, source_replica, source_slot
):
    replicas, tensors = lax.axis_size("replica"), lax.axis_size("tensor")
    z_size = replicas // X_SIZE
    x_groups = [[z * X_SIZE + x for x in range(X_SIZE)] for z in range(z_size)]
    z_groups = [[z * X_SIZE + x for z in range(z_size)] for x in range(X_SIZE)]
    steps, rows, model = queries.shape
    width = model // tensors
    rank = adapter_pages.shape[2]
    pages = X_SIZE * adapter_pages.shape[0]
    sr = steps * rows
    count = z_size * sr

    shrink_pages = lax.all_gather(
        adapter_pages[:, 0], "replica", axis_index_groups=x_groups, tiled=True
    )
    expand_pages = lax.all_gather(
        adapter_pages[:, 1], "replica", axis_index_groups=x_groups, tiled=True
    )

    parts = pl.pallas_call(
        attention_kernel,
        out_shape=jax.ShapeDtypeStruct((tensors, sr, width + LANES), bf16),
        in_specs=[smem_spec(), vmem_spec(), vmem_spec(), vmem_spec()],
        out_specs=vmem_spec(),
        scratch_shapes=[pltpu.VMEM((sr, model), f32)],
        compiler_params=params(),
        name="attention_part",
    )(lengths, queries, new_entries, cache)
    parts = lax.all_to_all(parts, "tensor", 0, 0, tiled=True)

    attended, outgoing = pl.pallas_call(
        combine_kernel,
        out_shape=(
            jax.ShapeDtypeStruct((steps, rows, width), bf16),
            jax.ShapeDtypeStruct((z_size, sr, width + LANES), bf16),
        ),
        in_specs=[smem_spec(), smem_spec(), smem_spec(), vmem_spec()],
        out_specs=(vmem_spec(), vmem_spec()),
        compiler_params=params(),
        name="combine",
    )(request_slots, source_replica[:, 0], source_slot, parts)
    column = lax.all_to_all(
        outgoing, "replica", 0, 0, tiled=True, axis_index_groups=z_groups
    )

    low = pl.pallas_call(
        shrink_kernel,
        out_shape=jax.ShapeDtypeStruct((tensors, count // 2, LANES), bf16),
        in_specs=[vmem_spec(), vmem_spec()],
        out_specs=vmem_spec(),
        compiler_params=params(),
        name="shrink_part",
    )(column, shrink_pages)
    low = lax.all_to_all(low, "tensor", 0, 0, tiled=True)

    back = pl.pallas_call(
        expand_kernel,
        out_shape=jax.ShapeDtypeStruct((z_size, sr, width), bf16),
        in_specs=[vmem_spec(), vmem_spec(), vmem_spec()],
        out_specs=vmem_spec(),
        compiler_params=params(),
        name="expand_rows",
    )(low, column, expand_pages)
    back = lax.all_to_all(back, "replica", 0, 0, tiled=True, axis_index_groups=z_groups)

    adapted = pl.pallas_call(
        gather_kernel,
        out_shape=jax.ShapeDtypeStruct((steps, rows, width), bf16),
        in_specs=[vmem_spec()],
        out_specs=vmem_spec(),
        compiler_params=params(),
        name="returned_rows",
    )(back)
    return attended, adapted


def solution(mesh):
    return jax.shard_map(
        per_device,
        mesh=mesh,
        in_specs=(
            P(None, "replica", None),
            P(None, "replica", None, None),
            P("replica", None, "tensor", None),
            P("replica"),
            P("replica", None, None, "tensor"),
            P("replica"),
            P("replica", None),
            P("replica"),
        ),
        out_specs=(P(None, "replica", "tensor"), P(None, "replica", "tensor")),
        check_vma=False,
    )
```

time: 296 us -> 116 us (0.39)
  waiting for transfers between devices: 106 us -> 27.5 us
  blocking collectives: 92.2 us -> 56.3 us
  other arithmetic: 35.1 us -> 0 us
  local copies, waits for them, and re-layouts: 35.6 us -> 5.56 us
  Pallas kernels: 0 us -> 7.2 us
  matrix products: 4.69 us -> 0 us
    all_to_all x1, waiting for transfers between devices: 106 us -> 0.01 us  [per_device(): low = lax.all_to_all(low, 'tensor', 0, 0, tiled=True)]
    all_to_all x0 -> x3, blocking collectives: none -> 56.3 us  [the longest x1 22.3 us: per_device(): parts = lax.all_to_all(parts, 'tensor', 0, 0, tiled=True)]
    all_gather x2 -> x0, blocking collectives: 38.6 us -> none  [joined(): everything = jax.tree.map(lambda part: lax.all_gather(part, axis), array)]
    psum x1 -> x0, blocking collectives: 30.5 us -> none  [per_device(): down_projection = lax.psum(shrink_part, 'tensor').astype(jnp.bfloat16)]
    all_gather x1 -> x2, waiting for transfers between devices: 0.02 us -> 26.8 us  [the longest x1 26.8 us: per_device(): lax.all_gather(adapter_pages[:, 1], 'replica', axis_index_groups=x_groups...]
    unnamed x1 -> x0, blocking collectives: 23.1 us -> none
    add x32 -> x0, other arithmetic: 20.1 us -> none  [the longest x15 19.6 us: joint(): accum_first * jnp.repeat(fade_first, spread, axis=-1)]
    gather x4 -> x0, local copies, waits for them, and re-layouts: 16.2 us -> none  [the longest x1 6.12 us: per_device(): inbox = jnp.take(flat_arrived, own_sources * CAP + rank_within, axis=0)]
  transfers between devices with their start and end apart: 2 -> 3, of which waited for: 1 -> 1; matrix products, arithmetic and copies ran while one was open for 17% -> 0% of each run, Pallas kernels for 0% -> 5%
where the time goes in v1:
time: 116 us; the launch traced here: 114 us
  blocking collectives  56.3 us (49%)
  waiting for transfers between devices  27.5 us (24%)
  between operations  14.2 us (12%)
  Pallas kernels  7.2 us (6%)
  local copies, waits for them, and re-layouts  5.56 us (5%)
  starting transfers between devices  3.8 us (3%)
    all_gather x1, waiting for transfers between devices, per_device(): lax.all_gather(adapter_pages[:, 1], 'replica', axis_index_groups=x_groups...  26.8 us
    all_to_all x1, blocking collectives, per_device(): parts = lax.all_to_all(parts, 'tensor', 0, 0, tiled=True)  22.3 us
    all_to_all x1, blocking collectives, per_device(): lax.all_to_all(outgoing, 'replica', 0, 0, tiled=True, axis_index_groups=z...  19.3 us
    all_to_all x1, blocking collectives, per_device(): lax.all_to_all(back, 'replica', 0, 0, tiled=True, axis_index_groups=z_gro...  14.7 us
    all_to_all x1, starting transfers between devices, per_device(): low = lax.all_to_all(low, 'tensor', 0, 0, tiled=True)  3.72 us
    unnamed x18, local copies, waits for them, and re-layouts  3.21 us
    pallas_call x1, Pallas kernels, per_device(): pl.pallas_call(attention_kernel, out_shape=jax.ShapeDtypeStruct((tensors,...  2.82 us
    slice x1, local copies, waits for them, and re-layouts, per_device(): adapter_pages[:, 1]  2.35 us
  transfers between devices with their start and end apart: 3, of which 1 were waited for; matrix products, arithmetic and copies ran while one was open for 0% of the time, Pallas kernels for 5%

profile of v1, /device:TPU:1, one launch (start us, length us, event | category | flops | bytes accessed | tf_op | source)
XLA Modules:
  0.0 114.5 jit_solution(1222587755837703229)
XLA Ops:
  7.2 0.0 copy-start.5
  7.2 0.0 copy-start.3
  7.2 0.0 copy-start.4
  7.2 0.0 copy-start.2
  7.2 0.0 copy-start.6
  7.2 0.0 copy-start.7
  7.2 0.0 copy-start.8
  7.2 0.0 all-gather.5.cloned.1.call-start
  7.3 2.3 %fusion = (bf16[8,1,64,512]{3,2,1,0:T(8,128)(2,1)}, bf16[8,1,64,512]{3,2,1,0:T(8,128)(2,1)}) fusion(bf16[8,2,64,512]{3,2,1,0:T(8,128)(2,1)} %param.12), kind=kLoop, calls=%fused_computation | loop fusion | bytes 2097152 | tf_op jit(solution)/shard_map/slice | solution.py:224
  9.6 0.0 all-gather.5.cloned.1.call-update
  9.7 0.0 all-gather.7.cloned.1.call-start
  9.7 0.7 all-gather.7.cloned.1.call-update
  10.4 0.0 copy-done.5
  10.4 0.0 copy-done.3
  10.4 0.0 copy-done.4
  10.4 0.0 copy-done.2
  10.4 2.8 %attention_part.1 = bf16[16,16,640]{2,1,0:T(8,128)(2,1)S(1)} custom-call(s32[4]{0:T(128)S(1)} %copy-done.5, bf16[4,4,8192]{2,1,0:T(4,128)(2,1)S(1)} %copy-done.3, bf16[4,4,8,256]{3,2,1,0:T(8,128)(2,1)S(1)} %copy-done.4, bf16[4,8,32,256]{3,2,1,0:T(8,128)(2,1)S(1)} %copy-done.2), custom_call_target="tpu_custom_call" | custom-call | tf_op jit(solution)/shard_map/attention_part/pallas_call | solution.py:227
  13.3 22.3 %all_to_all.20.part_ref = bf16[16,16,640]{2,1,0:T(8,128)(2,1)S(1)} all-to-all(bf16[16,16,640]{2,1,0:T(8,128)(2,1)S(1)} %attention_part.1), channel_id=1, replica_groups=mesh['replica'=32,'tensor'=16] {'tensor'}, dimensions={0} | all-to-all | bytes 655360 | tf_op jit(solution)/shard_map/all_to_all | solution.py:236
  35.6 0.0 copy-done.6
  35.6 0.0 copy-done.7
  35.6 0.0 copy-done.8
  35.6 1.6 %combine.1 = (bf16[4,4,512]{2,1,0:T(4,128)(2,1)}, bf16[8,16,640]{2,1,0:T(8,128)(2,1)S(1)}) custom-call(s32[4]{0:T(128)S(1)} %copy-done.6, s32[32]{0:T(128)S(1)} %bitcast.5, s32[32]{0:T(128)S(1)} %copy-done.8, bf16[16,16,640]{2,1,0:T(8,128)(2,1)S(1)} %all_to_all.20.part_ref), custom_call_target="tpu_custom_call" | custom-call | tf_op jit(solution)/shard_map/combine/pallas_call | solution.py:238
  37.2 19.3 %all_to_all.21.rows_ref = bf16[8,16,640]{2,1,0:T(8,128)(2,1)S(1)} all-to-all(bf16[8,16,640]{2,1,0:T(8,128)(2,1)S(1)} %get-tuple-element.5), channel_id=1, replica_groups={{0,64,128,192,256,320,384,448},{16,80,144,208,272,336,400,464},{32,96,1..., dimensions={0} | all-to-all | bytes 327680 | tf_op jit(solution)/shard_map/all_to_all | solution.py:249
  56.5 0.0 all-gather.5.cloned.1.call-done
  56.5 0.0 copy-start
  56.5 1.6 %copy-done = bf16[32,1,64,512]{3,2,1,0:T(8,128)(2,1)S(1)} copy-done((bf16[32,1,64,512]{3,2,1,0:T(8,128)(2,1)S(1)}, bf16[32,1,64,512]{3,2,1,0:T(8,128)(2,1)}, u32[]{:S(2)}) %copy-start) | copy-done | bytes 2097176
  58.1 1.6 %shrink_part.1 = bf16[16,64,128]{2,1,0:T(8,128)(2,1)} custom-call(bf16[8,16,640]{2,1,0:T(8,128)(2,1)S(1)} %all_to_all.21.rows_ref, bf16[32,64,512]{2,1,0:T(8,128)(2,1)S(1)} %bitcast.3), custom_call_target="tpu_custom_call" | custom-call | tf_op jit(solution)/shard_map/shrink_part/pallas_call | solution.py:253
  59.7 3.7 %all-to-all-start.2 = ((bf16[16,64,128]{2,1,0:T(8,128)(2,1)}), bf16[16,64,128]{2,1,0:T(8,128)(2,1)S(1)}, u32[]{:S(2)}, u32[]{:S(2)}) async-start(bf16[16,64,128]{2,1,0:T(8,128)(2,1)} %shrink_part.1), calls=%async_computation.2 | async-start | bytes 524288 | tf_op jit(solution)/shard_map/all_to_all | solution.py:261
  63.5 26.8 %all-gather.7.cloned.1.call-done = bf16[32,1,64,512]{3,2,1,0:T(8,128)(2,1)} async-done(((bf16[8,1,64,512]{3,2,1,0:T(8,128)(2,1)}), bf16[32,1,64,512]{3,2,1,0:T(8,128)(2,1)}) %all-gather.7.cloned.1.call-update) | async-done | bytes 2097168 | tf_op jit(solution)/shard_map/all_gather | solution.py:223
  90.2 0.0 all-to-all-done.2.part_ref
  90.2 0.0 copy-start.1
  90.2 1.6 %copy-done.1 = bf16[32,1,64,512]{3,2,1,0:T(8,128)(2,1)S(1)} copy-done((bf16[32,1,64,512]{3,2,1,0:T(8,128)(2,1)S(1)}, bf16[32,1,64,512]{3,2,1,0:T(8,128)(2,1)}, u32[]{:S(2)}) %copy-start.1) | copy-done | bytes 2097176
  91.8 0.5 expand_rows.1
  92.3 14.7 %all_to_all.22.part_ref = bf16[8,16,512]{2,1,0:T(8,128)(2,1)S(1)} all-to-all(bf16[8,16,512]{2,1,0:T(8,128)(2,1)S(1)} %expand_rows.1), channel_id=1, replica_groups={{0,64,128,192,256,320,384,448},{16,80,144,208,272,336,400,464},{32,96,1..., dimensions={0} | all-to-all | bytes 262144 | tf_op jit(solution)/shard_map/all_to_all | solution.py:271
  107.0 0.6 returned_rows.1
Async XLA Ops:
  7.2 3.2 %copy-start.5 = (s32[4]{0:T(128)S(1)}, s32[4]{0:T(128)}, u32[]{:S(2)}) copy-start(s32[4]{0:T(128)} %lengths_ref.1) | copy-start | bytes 52
  7.2 3.2 %copy-start.3 = (bf16[4,4,8192]{2,1,0:T(4,128)(2,1)S(1)}, bf16[4,4,8192]{2,1,0:T(4,128)(2,1)}, u32[]{:S(2)}) copy-start(bf16[4,4,8192]{2,1,0:T(4,128)(2,1)} %q_ref.1) | copy-start | bytes 786436
  7.2 3.2 %copy-start.4 = (bf16[4,4,8,256]{3,2,1,0:T(8,128)(2,1)S(1)}, bf16[4,4,8,256]{3,2,1,0:T(8,128)(2,1)}, u32[]{:S(2)}) copy-start(bf16[4,4,8,256]{3,2,1,0:T(8,128)(2,1)} %new_ref.1) | copy-start | bytes 196612
  7.2 3.2 %copy-start.2 = (bf16[4,8,32,256]{3,2,1,0:T(8,128)(2,1)S(1)}, bf16[4,8,32,256]{3,2,1,0:T(8,128)(2,1)}, u32[]{:S(2)}) copy-start(bf16[4,8,32,256]{3,2,1,0:T(8,128)(2,1)} %cache_ref.1) | copy-start | bytes 1572868
  7.2 28.4 %copy-start.6 = (s32[4]{0:T(128)S(1)}, s32[4]{0:T(128)}, u32[]{:S(2)}) copy-start(s32[4]{0:T(128)} %slots_ref.1) | copy-start | bytes 52
  7.2 28.4 %copy-start.7 = (s32[32,1]{0,1:T(1,128)S(1)}, s32[32,1]{0,1:T(1,128)}, u32[]{:S(2)}) copy-start(s32[32,1]{0,1:T(1,128)} %param.14) | copy-start | bytes 388
  7.2 28.4 %copy-start.8 = (s32[32]{0:T(128)S(1)}, s32[32]{0:T(128)}, u32[]{:S(2)}) copy-start(s32[32]{0:T(128)} %source_slot_ref.1) | copy-start | bytes 388
  7.2 49.3 %all-gather.5.cloned.1.call-start = ((), (), s32[]{:S(2)}) async-start(), calls=%async_computation.4 | async-start | bytes 2621440 | tf_op jit(solution)/shard_map/all_gather | solution.py:220
  9.7 80.6 %all-gather.7.cloned.1.call-start = ((), (), s32[]{:S(2)}) async-start(), calls=%async_computation.5 | async-start | bytes 2621440 | tf_op jit(solution)/shard_map/all_gather | solution.py:223
  56.5 1.6 %copy-start = (bf16[32,1,64,512]{3,2,1,0:T(8,128)(2,1)S(1)}, bf16[32,1,64,512]{3,2,1,0:T(8,128)(2,1)}, u32[]{:S(2)}) copy-start(bf16[32,1,64,512]{3,2,1,0:T(8,128)(2,1)} %all-gather.5.cloned.1.call-done) | copy-start | bytes 6291460
  59.7 30.5 %all-to-all-start.2 = ((bf16[16,64,128]{2,1,0:T(8,128)(2,1)}), bf16[16,64,128]{2,1,0:T(8,128)(2,1)S(1)}, u32[]{:S(2)}, u32[]{:S(2)}) async-start(bf16[16,64,128]{2,1,0:T(8,128)(2,1)} %shrink_part.1), calls=%async_computation.2 | async-start | bytes 524288 | tf_op jit(solution)/shard_map/all_to_all | solution.py:261
  90.2 1.6 %copy-start.1 = (bf16[32,1,64,512]{3,2,1,0:T(8,128)(2,1)S(1)}, bf16[32,1,64,512]{3,2,1,0:T(8,128)(2,1)}, u32[]{:S(2)}) copy-start(bf16[32,1,64,512]{3,2,1,0:T(8,128)(2,1)} %all-gather.7.cloned.1.call-done) | copy-start | bytes 6291460
Sparse Core Ops, SparseCore 0:
  10.2 41.6 all-gather.4
  53.9 36.2 all-gather.6

commit v2 on v1

--- a/solution.py
+++ b/solution.py
@@ -13,6 +13,7 @@
 ADAPTER_SCALE = 0.5
 NEG_LARGE = -1e30
 LANES = 128
+HELD = ((0, 0), (1, 0), (3, 0), (2, 0), (2, SLOTS // 2))
 
 
 def vmem_spec():
@@ -147,21 +148,28 @@
     return page[:, :1] == (first + iota((page.shape[0], width), 1) // rank).astype(f32)
 
 
-def shrink_kernel(rows_ref, shrink_ref, out_ref):
+def page_blocks(refs, half, at_once):
+    replica_here = lax.axis_index("replica")
+    z_here, x_here = replica_here // X_SIZE, replica_here % X_SIZE
+    for ref, (distance, start) in zip(refs, HELD):
+        owner = z_here * X_SIZE + jnp.bitwise_xor(x_here, distance)
+        for p in range(0, ref.shape[0], at_once):
+            block = ref[p : p + at_once, half]
+            yield owner * SLOTS + start + p, block.reshape(at_once * block.shape[1], block.shape[2])
+
+
+def shrink_kernel(rows_ref, *refs):
+    page_refs, out_ref = refs[:-1], refs[-1]
     z_count, rows, padded = rows_ref.shape
-    pages, rank, width = shrink_ref.shape
+    rank, width = page_refs[0].shape[2:]
     count = z_count * rows
     at_once = 256 // rank
     data = rows_ref[...].reshape(count, padded)
     x, page = data[:, :width], data[:, width:].astype(f32)
-    base = lax.axis_index("replica") // X_SIZE * (X_SIZE * SLOTS)
     accum = jnp.zeros((count, at_once * rank), f32)
-    for p in range(0, pages, at_once):
-        block = shrink_ref[p : p + at_once].reshape(at_once * rank, width)
+    for first, block in page_blocks(page_refs, 0, at_once):
         product = lax.dot_general(x, block, (((1,), (1,)), ((), ())), preferred_element_type=f32)
-        accum = accum + jnp.where(
-            page_columns(page, base + p, rank, at_once * rank), product, 0.0
-        )
+        accum = accum + jnp.where(page_columns(page, first, rank, at_once * rank), product, 0.0)
     folded = accum[:, :LANES] + accum[:, LANES:]
     folded = folded + pltpu.roll(folded, rank, 1)
     half = count // 2
@@ -170,13 +178,13 @@
         out_ref[t] = packed
 
 
-def expand_kernel(part_ref, rows_ref, expand_ref, out_ref):
+def expand_kernel(part_ref, rows_ref, *refs):
+    page_refs, out_ref = refs[:-1], refs[-1]
     z_count, rows, padded = rows_ref.shape
-    pages, rank, width = expand_ref.shape
+    rank, width = page_refs[0].shape[2:]
     count = z_count * rows
     at_once = 256 // rank
     page = rows_ref[:, :, width:].reshape(count, padded - width).astype(f32)
-    base = lax.axis_index("replica") // X_SIZE * (X_SIZE * SLOTS)
     packed = part_ref[0].astype(f32)
     for t in range(1, part_ref.shape[0]):
         packed = packed + part_ref[t].astype(f32)
@@ -187,9 +195,8 @@
     )
     low = jnp.concatenate([low, low], axis=1).astype(bf16).astype(f32)
     accum = jnp.zeros((count, width), f32)
-    for p in range(0, pages, at_once):
-        block = expand_ref[p : p + at_once].reshape(at_once * rank, width)
-        used = jnp.where(page_columns(page, base + p, rank, at_once * rank), low, 0.0)
+    for first, block in page_blocks(page_refs, 1, at_once):
+        used = jnp.where(page_columns(page, first, rank, at_once * rank), low, 0.0)
         accum = accum + jnp.dot(used.astype(bf16), block, preferred_element_type=f32)
     out_ref[...] = (accum * ADAPTER_SCALE).astype(bf16).reshape(z_count, rows, width)
 
@@ -208,21 +215,19 @@
 ):
     replicas, tensors = lax.axis_size("replica"), lax.axis_size("tensor")
     z_size = replicas // X_SIZE
-    x_groups = [[z * X_SIZE + x for x in range(X_SIZE)] for z in range(z_size)]
     z_groups = [[z * X_SIZE + x for z in range(z_size)] for x in range(X_SIZE)]
     steps, rows, model = queries.shape
     width = model // tensors
     rank = adapter_pages.shape[2]
-    pages = X_SIZE * adapter_pages.shape[0]
     sr = steps * rows
     count = z_size * sr
 
-    shrink_pages = lax.all_gather(
-        adapter_pages[:, 0], "replica", axis_index_groups=x_groups, tiled=True
-    )
-    expand_pages = lax.all_gather(
-        adapter_pages[:, 1], "replica", axis_index_groups=x_groups, tiled=True
-    )
+    def exchange(array, distance):
+        pairs = [(i, i // X_SIZE * X_SIZE + (i % X_SIZE ^ distance)) for i in range(replicas)]
+        return lax.ppermute(array, "replica", pairs)
+
+    beside = exchange(adapter_pages, 1)
+    before = exchange(adapter_pages, 3)
 
     parts = pl.pallas_call(
         attention_kernel,
@@ -234,6 +239,16 @@
         name="attention_part",
     )(lengths, queries, new_entries, cache)
     parts = lax.all_to_all(parts, "tensor", 0, 0, tiled=True)
+
+    half = SLOTS // 2
+    beside, before, _ = lax.optimization_barrier((beside, before, parts))
+    held = (
+        adapter_pages,
+        beside,
+        before,
+        exchange(before[:half], 1),
+        exchange(beside[half:], 3),
+    )
 
     attended, outgoing = pl.pallas_call(
         combine_kernel,
@@ -253,21 +268,21 @@
     low = pl.pallas_call(
         shrink_kernel,
         out_shape=jax.ShapeDtypeStruct((tensors, count // 2, LANES), bf16),
-        in_specs=[vmem_spec(), vmem_spec()],
+        in_specs=[vmem_spec()] * (1 + len(held)),
         out_specs=vmem_spec(),
         compiler_params=params(),
         name="shrink_part",
-    )(column, shrink_pages)
+    )(column, *held)
     low = lax.all_to_all(low, "tensor", 0, 0, tiled=True)
 
     back = pl.pallas_call(
         expand_kernel,
         out_shape=jax.ShapeDtypeStruct((z_size, sr, width), bf16),
-        in_specs=[vmem_spec(), vmem_spec(), vmem_spec()],
+        in_specs=[vmem_spec()] * (2 + len(held)),
         out_specs=vmem_spec(),
         compiler_params=params(),
         name="expand_rows",
-    )(low, column, expand_pages)
+    )(low, column, *held)
     back = lax.all_to_all(back, "replica", 0, 0, tiled=True, axis_index_groups=z_groups)
 
     adapted = pl.pallas_call(

time: 116 us -> 93.4 us (0.81)
  waiting for transfers between devices: 27.5 us -> 0.01 us
  between operations: 14.2 us -> 0.77 us
  blocking collectives: 56.3 us -> 68.3 us
  starting transfers between devices: 3.8 us -> 13.7 us
  local copies, waits for them, and re-layouts: 5.56 us -> 3.57 us
    all_gather x2 -> x0, waiting for transfers between devices: 26.8 us -> none  [the longest x1 26.8 us: per_device(): lax.all_gather(adapter_pages[:, 1], 'replica', axis_index_groups=x_groups...]
    all_to_all x0 -> x1, blocking collectives: none -> 16.9 us  [per_device(): low = lax.all_to_all(low, 'tensor', 0, 0, tiled=True)]
    ppermute x0 -> x4, starting transfers between devices: none -> 13.7 us  [exchange(): return lax.ppermute(array, 'replica', pairs)]
    all_to_all x1 -> x0, starting transfers between devices: 3.72 us -> none  [per_device(): low = lax.all_to_all(low, 'tensor', 0, 0, tiled=True)]
    all_to_all x1, blocking collectives: 14.7 us -> 12 us  [per_device(): lax.all_to_all(back, 'replica', 0, 0, tiled=True, axis_index_groups=z_gro...]
    slice x1 -> x2, local copies, waits for them, and re-layouts: 2.35 us -> 0.07 us  [the longest x1 0.04 us: per_device(): before[:half]]
    all_to_all x1, blocking collectives: 22.3 us -> 21.1 us  [per_device(): parts = lax.all_to_all(parts, 'tensor', 0, 0, tiled=True)]
    unnamed x18 -> x16, local copies, waits for them, and re-layouts: 3.21 us -> 3.5 us
  transfers between devices with their start and end apart: 3 -> 4, of which waited for: 1 -> 0; matrix products, arithmetic and copies ran while one was open for 0% -> 0% of each run, Pallas kernels for 5% -> 5%
where the time goes in v2:
time: 93.4 us; the launch traced here: 92.9 us
  blocking collectives  68.3 us (73%)
  starting transfers between devices  13.7 us (15%)
  Pallas kernels  6.5 us (7%)
  local copies, waits for them, and re-layouts  3.57 us (4%)
    all_to_all x1, blocking collectives, per_device(): parts = lax.all_to_all(parts, 'tensor', 0, 0, tiled=True)  21.1 us
    all_to_all x1, blocking collectives, per_device(): lax.all_to_all(outgoing, 'replica', 0, 0, tiled=True, axis_index_groups=z...  18.3 us
    all_to_all x1, blocking collectives, per_device(): low = lax.all_to_all(low, 'tensor', 0, 0, tiled=True)  16.9 us
    ppermute x4, starting transfers between devices, exchange(): return lax.ppermute(array, 'replica', pairs)  13.7 us
    all_to_all x1, blocking collectives, per_device(): lax.all_to_all(back, 'replica', 0, 0, tiled=True, axis_index_groups=z_gro...  12 us
    unnamed x16, local copies, waits for them, and re-layouts  3.5 us
    pallas_call x1, Pallas kernels, per_device(): pl.pallas_call(attention_kernel, out_shape=jax.ShapeDtypeStruct((tensors,...  2.83 us
  transfers between devices with their start and end apart: 4, of which 0 were waited for; matrix products, arithmetic and copies ran while one was open for 0% of the time, Pallas kernels for 5%

profile of v2, /device:TPU:1, one launch (start us, length us, event | category | flops | bytes accessed | tf_op | source)
XLA Modules:
  0.0 92.9 jit_solution(10423664512351176854)
XLA Ops:
  0.6 5.2 %collective-permute-start.1 = (bf16[8,2,64,512]{3,2,1,0:T(8,128)(2,1)}, bf16[8,2,64,512]{3,2,1,0:T(8,128)(2,1)S(1)}, u32[]{:S(2)}, u32[]{:S(2)}) collective-permute-start(bf16[8,2,64,512]{3,2,1,0:T(8,128)(2,1)} %refs_0_.3), channel_id=1, source_target_pairs={{0,48},{16,32},{32,16},{48,0},{64,112},{80,96},{96,80},{112,64},{1... | collective-permute-start | bytes 3145736 | tf_op jit(solution)/shard_map/ppermute | solution.py:227
  5.9 1.9 %collective-permute-start = (bf16[8,2,64,512]{3,2,1,0:T(8,128)(2,1)}, bf16[8,2,64,512]{3,2,1,0:T(8,128)(2,1)S(1)}, u32[]{:S(2)}, u32[]{:S(2)}) collective-permute-start(bf16[8,2,64,512]{3,2,1,0:T(8,128)(2,1)} %refs_0_.3), channel_id=1, source_target_pairs={{0,16},{16,0},{32,48},{48,32},{64,80},{80,64},{96,112},{112,96},{1... | collective-permute-start | bytes 3145736 | tf_op jit(solution)/shard_map/ppermute | solution.py:227
  7.8 0.0 copy-start.1
  7.8 1.0 %copy-done.1 = bf16[4,8,32,256]{3,2,1,0:T(8,128)(2,1)S(1)} copy-done((bf16[4,8,32,256]{3,2,1,0:T(8,128)(2,1)S(1)}, bf16[4,8,32,256]{3,2,1,0:T(8,128)(2,1)}, u32[]{:S(2)}) %copy-start.1) | copy-done | bytes 524312
  8.8 0.0 copy-start.2
  8.8 0.9 %copy-done.2 = bf16[4,4,8192]{2,1,0:T(4,128)(2,1)S(1)} copy-done((bf16[4,4,8192]{2,1,0:T(4,128)(2,1)S(1)}, bf16[4,4,8192]{2,1,0:T(4,128)(2,1)}, u32[]{:S(2)}) %copy-start.2) | copy-done | bytes 262168
  9.8 0.0 copy-start.3
  9.8 0.8 copy-done.3
  10.6 0.0 copy-start.4
  10.6 0.7 copy-done.4
  11.3 2.8 %attention_part.1 = bf16[16,16,640]{2,1,0:T(8,128)(2,1)S(1)} custom-call(s32[4]{0:T(128)S(1)} %copy-done.4, bf16[4,4,8192]{2,1,0:T(4,128)(2,1)S(1)} %copy-done.2, bf16[4,4,8,256]{3,2,1,0:T(8,128)(2,1)S(1)} %copy-done.3, bf16[4,8,32,256]{3,2,1,0:T(8,128)(2,1)S(1)} %copy-done.1), custom_call_target="tpu_custom_call" | custom-call | tf_op jit(solution)/shard_map/attention_part/pallas_call | solution.py:232
  14.1 21.1 %all_to_all.20.part_ref = bf16[16,16,640]{2,1,0:T(8,128)(2,1)S(1)} all-to-all(bf16[16,16,640]{2,1,0:T(8,128)(2,1)S(1)} %attention_part.1), channel_id=1, replica_groups=mesh['replica'=32,'tensor'=16] {'tensor'}, dimensions={0} | all-to-all | bytes 655360 | tf_op jit(solution)/shard_map/all_to_all | solution.py:241
  35.3 0.0 collective-permute-done.1.refs_2_
  35.3 0.0 collective-permute-done.refs_1_
  35.3 0.0 copy-start
  35.4 0.0 copy-start.5
  35.4 0.0 copy-start.6
  35.4 0.0 copy-start.7
  35.4 3.6 %collective-permute-start.2 = (bf16[4,2,64,512]{3,2,1,0:T(8,128)(2,1)S(1)}, bf16[4,2,64,512]{3,2,1,0:T(8,128)(2,1)S(1)}, u32[]{:S(2)}, u32[]{:S(2)}) collective-permute-start(bf16[4,2,64,512]{3,2,1,0:T(8,128)(2,1)S(1)} %slice.6), channel_id=1, source_target_pairs={{0,16},{16,0},{32,48},{48,32},{64,80},{80,64},{96,112},{112,96},{1... | collective-permute-start | bytes 1572872 | tf_op jit(solution)/shard_map/ppermute | solution.py:227
  39.0 3.0 %collective-permute-start.3 = (bf16[4,2,64,512]{3,2,1,0:T(8,128)(2,1)S(1)}, bf16[4,2,64,512]{3,2,1,0:T(8,128)(2,1)S(1)}, u32[]{:S(2)}, u32[]{:S(2)}) collective-permute-start(bf16[4,2,64,512]{3,2,1,0:T(8,128)(2,1)S(1)} %slice.7), channel_id=1, source_target_pairs={{0,48},{16,32},{32,16},{48,0},{64,112},{80,96},{96,80},{112,64},{1... | collective-permute-start | bytes 1572872 | tf_op jit(solution)/shard_map/ppermute | solution.py:227
  41.9 0.0 copy-done.5
  41.9 0.0 copy-done.6
  42.0 0.0 copy-done.7
  42.0 1.6 %combine.1 = (bf16[4,4,512]{2,1,0:T(4,128)(2,1)}, bf16[8,16,640]{2,1,0:T(8,128)(2,1)S(1)}) custom-call(s32[4]{0:T(128)S(1)} %copy-done.5, s32[32]{0:T(128)S(1)} %bitcast.1, s32[32]{0:T(128)S(1)} %copy-done.7, bf16[16,16,640]{2,1,0:T(8,128)(2,1)S(1)} %all_to_all.20.part_ref), custom_call_target="tpu_custom_call" | custom-call | tf_op jit(solution)/shard_map/combine/pallas_call | solution.py:253
  43.6 18.3 %all_to_all.21.rows_ref = bf16[8,16,640]{2,1,0:T(8,128)(2,1)S(1)} all-to-all(bf16[8,16,640]{2,1,0:T(8,128)(2,1)S(1)} %get-tuple-element.7), channel_id=1, replica_groups={{0,64,128,192,256,320,384,448},{16,80,144,208,272,336,400,464},{32,96,1..., dimensions={0} | all-to-all | bytes 327680 | tf_op jit(solution)/shard_map/all_to_all | solution.py:264
  61.9 0.0 collective-permute-done.2.refs_3_
  61.9 0.0 collective-permute-done.3.refs_4_
  61.9 0.0 copy-done
  61.9 0.9 shrink_part.1
  62.8 16.9 %all_to_all.22.part_ref = bf16[16,64,128]{2,1,0:T(8,128)(2,1)S(1)} all-to-all(bf16[16,64,128]{2,1,0:T(8,128)(2,1)S(1)} %shrink_part.1), channel_id=1, replica_groups=mesh['replica'=32,'tensor'=16] {'tensor'}, dimensions={0} | all-to-all | bytes 524288 | tf_op jit(solution)/shard_map/all_to_all | solution.py:276
  79.7 0.5 expand_rows.1
  80.3 12.0 %all_to_all.23.part_ref = bf16[8,16,512]{2,1,0:T(8,128)(2,1)S(1)} all-to-all(bf16[8,16,512]{2,1,0:T(8,128)(2,1)S(1)} %expand_rows.1), channel_id=1, replica_groups={{0,64,128,192,256,320,384,448},{16,80,144,208,272,336,400,464},{32,96,1..., dimensions={0} | all-to-all | bytes 262144 | tf_op jit(solution)/shard_map/all_to_all | solution.py:286
  92.2 0.6 returned_rows.1
  (2 shorter events, 0.1 us)
Async XLA Ops:
  0.6 34.6 %collective-permute-start.1 = (bf16[8,2,64,512]{3,2,1,0:T(8,128)(2,1)}, bf16[8,2,64,512]{3,2,1,0:T(8,128)(2,1)S(1)}, u32[]{:S(2)}, u32[]{:S(2)}) collective-permute-start(bf16[8,2,64,512]{3,2,1,0:T(8,128)(2,1)} %refs_0_.3), channel_id=1, source_target_pairs={{0,48},{16,32},{32,16},{48,0},{64,112},{80,96},{96,80},{112,64},{1... | collective-permute-start | bytes 3145736 | tf_op jit(solution)/shard_map/ppermute | solution.py:227
  5.9 29.4 %collective-permute-start = (bf16[8,2,64,512]{3,2,1,0:T(8,128)(2,1)}, bf16[8,2,64,512]{3,2,1,0:T(8,128)(2,1)S(1)}, u32[]{:S(2)}, u32[]{:S(2)}) collective-permute-start(bf16[8,2,64,512]{3,2,1,0:T(8,128)(2,1)} %refs_0_.3), channel_id=1, source_target_pairs={{0,16},{16,0},{32,48},{48,32},{64,80},{80,64},{96,112},{112,96},{1... | collective-permute-start | bytes 3145736 | tf_op jit(solution)/shard_map/ppermute | solution.py:227
  7.8 1.0 %copy-start.1 = (bf16[4,8,32,256]{3,2,1,0:T(8,128)(2,1)S(1)}, bf16[4,8,32,256]{3,2,1,0:T(8,128)(2,1)}, u32[]{:S(2)}) copy-start(bf16[4,8,32,256]{3,2,1,0:T(8,128)(2,1)} %cache_ref.1) | copy-start | bytes 1572868
  8.8 0.9 %copy-start.2 = (bf16[4,4,8192]{2,1,0:T(4,128)(2,1)S(1)}, bf16[4,4,8192]{2,1,0:T(4,128)(2,1)}, u32[]{:S(2)}) copy-start(bf16[4,4,8192]{2,1,0:T(4,128)(2,1)} %q_ref.1) | copy-start | bytes 786436
  9.8 0.8 copy-start.3
  10.6 0.7 copy-start.4
  35.3 26.6 %copy-start = (bf16[8,2,64,512]{3,2,1,0:T(8,128)(2,1)S(1)}, bf16[8,2,64,512]{3,2,1,0:T(8,128)(2,1)}, u32[]{:S(2)}) copy-start(bf16[8,2,64,512]{3,2,1,0:T(8,128)(2,1)} %refs_0_.3) | copy-start | bytes 3145732
  35.4 6.6 %copy-start.5 = (s32[4]{0:T(128)S(1)}, s32[4]{0:T(128)}, u32[]{:S(2)}) copy-start(s32[4]{0:T(128)} %slots_ref.1) | copy-start | bytes 52
  35.4 6.6 %copy-start.6 = (s32[32,1]{0,1:T(1,128)S(1)}, s32[32,1]{0,1:T(1,128)}, u32[]{:S(2)}) copy-start(s32[32,1]{0,1:T(1,128)} %param.14) | copy-start | bytes 388
  35.4 6.6 %copy-start.7 = (s32[32]{0:T(128)S(1)}, s32[32]{0:T(128)}, u32[]{:S(2)}) copy-start(s32[32]{0:T(128)} %source_slot_ref.1) | copy-start | bytes 388
  35.4 26.5 %collective-permute-start.2 = (bf16[4,2,64,512]{3,2,1,0:T(8,128)(2,1)S(1)}, bf16[4,2,64,512]{3,2,1,0:T(8,128)(2,1)S(1)}, u32[]{:S(2)}, u32[]{:S(2)}) collective-permute-start(bf16[4,2,64,512]{3,2,1,0:T(8,128)(2,1)S(1)} %slice.6), channel_id=1, source_target_pairs={{0,16},{16,0},{32,48},{48,32},{64,80},{80,64},{96,112},{112,96},{1... | collective-permute-start | bytes 1572872 | tf_op jit(solution)/shard_map/ppermute | solution.py:227
  39.0 22.9 %collective-permute-start.3 = (bf16[4,2,64,512]{3,2,1,0:T(8,128)(2,1)S(1)}, bf16[4,2,64,512]{3,2,1,0:T(8,128)(2,1)S(1)}, u32[]{:S(2)}, u32[]{:S(2)}) collective-permute-start(bf16[4,2,64,512]{3,2,1,0:T(8,128)(2,1)S(1)} %slice.7), channel_id=1, source_target_pairs={{0,48},{16,32},{32,16},{48,0},{64,112},{80,96},{96,80},{112,64},{1... | collective-permute-start | bytes 1572872 | tf_op jit(solution)/shard_map/ppermute | solution.py:227

commit v3 on v2

v3 whole, which is shorter than its diff:
```python
import jax
import jax.numpy as jnp
from jax import lax
from jax.experimental import pallas as pl
from jax.experimental.pallas import tpu as pltpu
from jax.sharding import PartitionSpec as P

f32 = jnp.float32
bf16 = jnp.bfloat16

X_SIZE = 4
SLOTS = 8
ADAPTER_SCALE = 0.5
NEG_LARGE = -1e30
LANES = 128
LOG2_E = 1.4426950408889634
BLOCK = (0, 1, 3, 2)
ROWS = 4
AT_ONCE = 16


def vmem_spec():
    return pl.BlockSpec(memory_space=pltpu.VMEM)


def hbm_spec():
    return pl.BlockSpec(memory_space=pltpu.HBM)


def in_hbm(array):
    return pltpu.with_memory_space_constraint(array, pltpu.HBM)


def smem_spec():
    return pl.BlockSpec(memory_space=pltpu.SMEM)


def params():
    return pltpu.CompilerParams(vmem_limit_bytes=8 * 1024 * 1024)


def iota(shape, axis):
    return lax.broadcasted_iota(jnp.int32, shape, axis)


def attention_kernel(
    lengths_hbm,
    q_hbm,
    new_hbm,
    cache_hbm,
    out_hbm,
    lengths_ref,
    q_ref,
    new_ref,
    cache_ref,
    q_rows,
    out_ref,
    arrived,
    sent,
):
    copies = [
        pltpu.make_async_copy(q_hbm, q_ref, arrived.at[0]),
        pltpu.make_async_copy(new_hbm, new_ref, arrived.at[1]),
        pltpu.make_async_copy(lengths_hbm, lengths_ref, arrived.at[2]),
    ]
    cache_copies = [
        pltpu.make_async_copy(cache_hbm.at[:, g], cache_ref.at[g], arrived.at[3 + g])
        for g in range(cache_ref.shape[0])
    ]
    for copy in copies + cache_copies:
        copy.start()
    steps, rows, width = q_ref.shape
    kv_heads, local = cache_ref.shape[0], cache_ref.shape[2]
    head = cache_ref.shape[3] // 2
    group = width // head // kv_heads
    tensor_here = lax.axis_index("tensor")
    sr = steps * rows
    count = group * sr
    shape = (count, rows * local)
    row_id, col_id = iota(shape, 0), iota(shape, 1)
    request, col_request = row_id % rows, col_id // local
    fresh_shape = (count, steps * rows * kv_heads)
    fresh_row, fresh_col = iota(fresh_shape, 0), iota(fresh_shape, 1)
    fresh = (
        (fresh_row % rows == (fresh_col // kv_heads) % rows)
        & (fresh_col // (kv_heads * rows) <= (fresh_row // rows) % steps)
        & (tensor_here == 0)
    )
    fresh_head = jnp.where(fresh, fresh_col % kv_heads, -1)
    lane = iota((sr, LANES), 1)
    per_tile = out_ref.shape[2] // head - 1
    field = LANES // 2 // per_tile
    factor = head ** (-0.5) * LOG2_E
    contract = (((1,), (1,)), ((), ()))
    for copy in copies + cache_copies:
        copy.wait()
    length = jnp.zeros(shape, jnp.int32)
    for r in range(rows):
        length = jnp.where(col_request == r, lengths_ref[r], length)
    visible = (request == col_request) & (tensor_here * local + col_id % local < length)
    for s in range(steps):
        q_rows[s * rows : (s + 1) * rows, :] = q_ref[s].astype(f32)
    new_all = new_ref[...].astype(f32).reshape(steps * rows * kv_heads, 2 * head).astype(bf16)
    new_keys, new_values = new_all[:, :head], new_all[:, head:]
    ones = jnp.ones((rows * local + new_keys.shape[0], head), bf16)
    out_copies = []
    for g in range(kv_heads):
        q = jnp.concatenate(
            [q_rows[:, (g * group + k) * head : (g * group + k + 1) * head] for k in range(group)],
            axis=0,
        ).astype(bf16)
        keys = cache_ref[g, :, :, :head].reshape(rows * local, head)
        values = cache_ref[g, :, :, head:].reshape(rows * local, head)
        keys = jnp.concatenate([keys, new_keys], axis=0)
        values = jnp.concatenate([values, new_values], axis=0)
        values = jnp.concatenate([values, ones], axis=1)
        scores = lax.dot_general(q, keys, contract, preferred_element_type=f32) * factor
        old_scores = jnp.where(visible, scores[:, : rows * local], NEG_LARGE)
        new_scores = jnp.where(fresh_head == g, scores[:, rows * local :], NEG_LARGE)
        top = jnp.max(jnp.maximum(old_scores, new_scores), axis=1, keepdims=True)
        shift = jnp.maximum(top, 0.01 * NEG_LARGE).astype(bf16).astype(f32)
        weights = jnp.concatenate(
            [jnp.exp2(old_scores - shift), jnp.exp2(new_scores - shift)], axis=1
        ).astype(bf16)
        sums = jnp.dot(weights, values, preferred_element_type=f32)
        accum, total = sums[:, :head], sums[:, head:]
        for first in range(0, group, per_tile):
            place = (g * group + first) // per_tile
            stats = jnp.zeros((sr, LANES), f32)
            for k in range(per_tile):
                part = slice((first + k) * sr, (first + k + 1) * sr)
                out_ref[place, :, k * head : (k + 1) * head] = accum[part].astype(bf16)
                stats = jnp.where(lane // field == k, shift[part], stats)
                stats = jnp.where(lane // field == per_tile + k, total[part], stats)
            out_ref[place, :, per_tile * head :] = stats.astype(bf16)
        places = group // per_tile
        here = pl.ds(g * places, places)
        out_copies.append(
            pltpu.make_async_copy(out_ref.at[here], out_hbm.at[here], sent.at[g])
        )
        out_copies[-1].start()
    for copy in out_copies:
        copy.wait()


def send_all(ref, hbm, sent):
    copies = [
        pltpu.make_async_copy(ref, hbm.at[i], sent.at[i]) for i in range(hbm.shape[0])
    ]
    for copy in copies:
        copy.start()
    for copy in copies:
        copy.wait()


def combine_kernel(slots_ref, source_ref, source_slot_ref, part_ref, attended_ref, send_hbm, send_ref, sent):
    steps, rows, width = attended_ref.shape
    sources = part_ref.shape[0]
    per_tile = width // LANES
    field = LANES // 2 // per_tile
    stats = [part_ref[t, :, width:].astype(f32) for t in range(sources)]
    top = stats[0]
    for t in range(1, sources):
        top = jnp.maximum(top, stats[t])
    sums = [jnp.zeros((steps * rows, LANES), f32) for _ in range(per_tile)]
    total = jnp.zeros((steps * rows, LANES), f32)
    for t in range(sources):
        fade = jnp.exp2(stats[t] - top)
        total = total + fade * pltpu.roll(stats[t], LANES // 2, 1)
        for k in range(per_tile):
            sums[k] = sums[k] + fade[:, k * field : k * field + 1] * part_ref[
                t, :, k * LANES : (k + 1) * LANES
            ].astype(f32)
    replica_here = lax.axis_index("replica")
    row = iota((steps * rows, LANES), 0) % rows
    page = jnp.zeros((steps * rows, LANES), f32)
    for r in range(rows):
        slot = slots_ref[r]
        entry = jnp.clip(slot - SLOTS, 0, source_slot_ref.shape[0] - 1)
        number = jnp.where(
            slot < SLOTS,
            replica_here * SLOTS + slot,
            source_ref[entry] * SLOTS + source_slot_ref[entry],
        )
        page = jnp.where(row == r, number.astype(f32), page)
    page = page.astype(bf16)
    for k in range(per_tile):
        attended = sums[k] / total[:, k * field : k * field + 1]
        for s in range(steps):
            attended_ref[s, :, k * LANES : (k + 1) * LANES] = attended[
                s * rows : (s + 1) * rows
            ].astype(bf16)
        rounded = attended.astype(bf16)
        send_ref[:, k * LANES : (k + 1) * LANES] = rounded
    send_ref[:, width:] = page
    send_all(send_ref, send_hbm, sent)


def page_columns(page, first, rank, width):
    return page[:, :1] == (first + iota((page.shape[0], width), 1) // rank).astype(f32)


def page_blocks(refs, at_once):
    replica_here = lax.axis_index("replica")
    for distance, ref in zip(BLOCK, refs):
        first = jnp.bitwise_xor(replica_here, distance) * SLOTS
        for p in range(0, ref.shape[0], at_once):
            block = ref[p : p + at_once]
            yield first + p, block.reshape(at_once * block.shape[1], block.shape[2])


def shrink_kernel(
    turn_ref,
    rows_ref,
    *refs,
):
    members, steps_rows, padded = rows_ref.shape
    page_refs = refs[: len(BLOCK)]
    out_hbm, place_ref, chosen_ref, count_ref, out_ref, sent = refs[len(BLOCK) :]
    rank, width = page_refs[0].shape[1:]
    count = members * steps_rows
    rows = ROWS
    steps = steps_rows // rows
    data = rows_ref[...].reshape(count, padded)
    x, page = data[:, :width], data[:, width:].astype(f32)
    distance = jnp.bitwise_xor(page.astype(jnp.int32) // SLOTS, lax.axis_index("replica"))
    held = distance == BLOCK[0]
    for other in BLOCK[1:]:
        held = held | (distance == other)
    held = held.astype(f32)
    one, other = iota((count, count), 0), iota((count, count), 1)
    earlier = (
        (other // steps_rows * rows + other % rows < one // steps_rows * rows + one % rows)
        & (other % steps_rows < rows)
    ).astype(f32).astype(bf16)
    order = jnp.dot(earlier, held.astype(bf16), preferred_element_type=f32)
    row = iota((count, LANES), 0)
    lane = iota((count, LANES), 1)
    slots = AT_ONCE * steps
    wanted = turn_ref[0] * AT_ONCE + lane // steps
    place = (
        (held > 0.0)
        & (order == wanted.astype(f32))
        & (row % steps_rows // rows == lane % steps)
        & (lane < slots)
    ).astype(f32).astype(bf16)
    place_ref[...] = place
    count_ref[0] = jnp.sum(
        jnp.where((row % steps_rows < rows) & (lane == 0), held, 0.0)
    ).astype(jnp.int32)
    down = (((0,), (0,)), ((), ()))
    x = lax.dot_general(place[:, :slots], x, down, preferred_element_type=f32).astype(bf16)
    page = lax.dot_general(place[:, :slots], data[:, width:], down, preferred_element_type=f32)
    chosen_ref[...] = page
    at_once = 256 // rank
    accum = jnp.zeros((slots, at_once * rank), f32)
    for first, block in page_blocks(page_refs, at_once):
        product = lax.dot_general(x, block, (((1,), (1,)), ((), ())), preferred_element_type=f32)
        accum = accum + jnp.where(page_columns(page, first, rank, at_once * rank), product, 0.0)
    folded = accum[:, :LANES] + accum[:, LANES:]
    folded = folded + pltpu.roll(folded, rank, 1)
    half = slots // 2
    packed = jnp.where(iota((half, LANES), 1) < rank, folded[:half], folded[half:]).astype(bf16)
    out_ref[...] = packed
    send_all(out_ref, out_hbm, sent)


def expand_kernel(part_ref, place_ref, chosen_ref, *refs):
    page_refs, out_ref = refs[:-1], refs[-1]
    members, steps_rows, width = out_ref.shape
    rank = page_refs[0].shape[1]
    slots = chosen_ref.shape[0]
    page = chosen_ref[...]
    packed = part_ref[0].astype(f32)
    for t in range(1, part_ref.shape[0]):
        packed = packed + part_ref[t].astype(f32)
    swapped = pltpu.roll(packed, rank, 1)
    left = iota(packed.shape, 1) < rank
    low = jnp.concatenate(
        [jnp.where(left, packed, swapped), jnp.where(left, swapped, packed)], axis=0
    )
    low = jnp.concatenate([low, low], axis=1).astype(bf16).astype(f32)
    at_once = 256 // rank
    accum = jnp.zeros((slots, width), f32)
    for first, block in page_blocks(page_refs, at_once):
        used = jnp.where(page_columns(page, first, rank, at_once * rank), low, 0.0)
        accum = accum + jnp.dot(used.astype(bf16), block, preferred_element_type=f32)
    result = (accum * ADAPTER_SCALE).astype(bf16)
    spread = jnp.dot(place_ref[:, :slots], result, preferred_element_type=f32).astype(bf16)
    out_ref[...] = spread.reshape(members, steps_rows, width)


def gather_kernel(part_ref, out_ref):
    steps, rows, _ = out_ref.shape
    total = part_ref[0].astype(f32)
    for z in range(1, part_ref.shape[0]):
        total = total + part_ref[z].astype(f32)
    for s in range(steps):
        out_ref[s] = total[s * rows : (s + 1) * rows].astype(bf16)


def per_device(
    queries, new_entries, cache, lengths, adapter_pages, request_slots, source_replica, source_slot
):
    replicas, tensors = lax.axis_size("replica"), lax.axis_size("tensor")
    z_size = replicas // X_SIZE
    groups = [[z * X_SIZE + x for z in range(z_size)] for x in range(X_SIZE)]
    members = len(groups[0])
    steps, rows, model = queries.shape
    width = model // tensors
    kv_heads = cache.shape[1]
    rank = adapter_pages.shape[2]
    sr = steps * rows
    count = members * sr

    def exchange(array, distance):
        return lax.ppermute(array, "replica", [(i, i ^ distance) for i in range(replicas)])

    shrink_own, expand_own = adapter_pages[:, 0], adapter_pages[:, 1]
    shrink_pages = [shrink_own] + [exchange(shrink_own, d) for d in BLOCK[1:]]
    expand_pages = [expand_own] + [exchange(expand_own, d) for d in BLOCK[1:]]

    parts = pl.pallas_call(
        attention_kernel,
        out_shape=pltpu.HBM((tensors, sr, width + LANES), bf16),
        in_specs=[hbm_spec()] * 4,
        out_specs=hbm_spec(),
        scratch_shapes=[
            pltpu.SMEM(lengths.shape, lengths.dtype),
            pltpu.VMEM(queries.shape, bf16),
            pltpu.VMEM(new_entries.shape, bf16),
            pltpu.VMEM((kv_heads,) + cache.shape[:1] + cache.shape[2:], bf16),
            pltpu.VMEM((sr, model), f32),
            pltpu.VMEM((tensors, sr, width + LANES), bf16),
            pltpu.SemaphoreType.DMA((3 + kv_heads,)),
            pltpu.SemaphoreType.DMA((kv_heads,)),
        ],
        compiler_params=params(),
        name="attention_part",
    )(*[in_hbm(array) for array in (lengths, queries, new_entries, cache)])
    parts = lax.all_to_all(parts, "tensor", 0, 0, tiled=True)

    attended, outgoing = pl.pallas_call(
        combine_kernel,
        out_shape=(
            jax.ShapeDtypeStruct((steps, rows, width), bf16),
            pltpu.HBM((members, sr, width + LANES), bf16),
        ),
        in_specs=[smem_spec(), smem_spec(), smem_spec(), vmem_spec()],
        out_specs=(vmem_spec(), hbm_spec()),
        scratch_shapes=[
            pltpu.VMEM((sr, width + LANES), bf16),
            pltpu.SemaphoreType.DMA((members,)),
        ],
        compiler_params=params(),
        name="combine",
    )(request_slots, source_replica[:, 0], source_slot, parts)
    column = lax.all_to_all(
        outgoing, "replica", 0, 0, tiled=True, axis_index_groups=groups
    )

    slots = AT_ONCE * steps

    def turn(k):
        low, place, chosen, held = pl.pallas_call(
            shrink_kernel,
            out_shape=(
                pltpu.HBM((tensors, slots // 2, LANES), bf16),
                jax.ShapeDtypeStruct((count, LANES), bf16),
                jax.ShapeDtypeStruct((slots, LANES), f32),
                jax.ShapeDtypeStruct((1,), jnp.int32),
            ),
            in_specs=[smem_spec()] + [vmem_spec()] * (1 + len(BLOCK)),
            out_specs=(hbm_spec(), vmem_spec(), vmem_spec(), smem_spec()),
            scratch_shapes=[
                pltpu.VMEM((slots // 2, LANES), bf16),
                pltpu.SemaphoreType.DMA((tensors,)),
            ],
            compiler_params=params(),
            name="shrink_part",
        )(jnp.full((1,), k, jnp.int32), column, *shrink_pages)
        low = lax.all_to_all(low, "tensor", 0, 0, tiled=True)
        back = pl.pallas_call(
            expand_kernel,
            out_shape=jax.ShapeDtypeStruct((members, sr, width), bf16),
            in_specs=[vmem_spec()] * (3 + len(BLOCK)),
            out_specs=vmem_spec(),
            compiler_params=params(),
            name="expand_rows",
        )(low, place, chosen, *expand_pages)
        return back, held[0]

    back, held = turn(0)
    _, back = lax.while_loop(
        lambda state: state[0] * AT_ONCE < held,
        lambda state: (state[0] + 1, state[1] + turn(state[0])[0]),
        (jnp.int32(1), back),
    )
    back = lax.all_to_all(back, "replica", 0, 0, tiled=True, axis_index_groups=groups)

    adapted = pl.pallas_call(
        gather_kernel,
        out_shape=jax.ShapeDtypeStruct((steps, rows, width), bf16),
        in_specs=[vmem_spec()],
        out_specs=vmem_spec(),
        compiler_params=params(),
        name="returned_rows",
    )(back)
    return attended, adapted


def solution(mesh):
    return jax.shard_map(
        per_device,
        mesh=mesh,
        in_specs=(
            P(None, "replica", None),
            P(None, "replica", None, None),
            P("replica", None, "tensor", None),
            P("replica"),
            P("replica", None, None, "tensor"),
            P("replica"),
            P("replica", None),
            P("replica"),
        ),
        out_specs=(P(None, "replica", "tensor"), P(None, "replica", "tensor")),
        check_vma=False,
    )
```

time: 93.4 us -> 85.6 us (0.916)
  blocking collectives: 68.3 us -> 14.9 us
  starting transfers between devices: 13.7 us -> 41.3 us
  waiting for transfers between devices: 0.01 us -> 15.5 us
  Pallas kernels: 6.5 us -> 10.8 us
  local copies, waits for them, and re-layouts: 3.57 us -> 0.11 us
    all_to_all x4 -> x1, blocking collectives: 68.3 us -> 14.9 us  [per_device(): lax.all_to_all(back, 'replica', 0, 0, tiled=True, axis_index_groups=groups)]
    all_to_all x0 -> x3, starting transfers between devices: none -> 23.4 us  [the longest x1 10.2 us: per_device(): parts = lax.all_to_all(parts, 'tensor', 0, 0, tiled=True)]
    ppermute x4 -> x6, waiting for transfers between devices: 0.01 us -> 10.1 us  [exchange(): lax.ppermute(array, 'replica', [(i, i ^ distance) for i in range(replicas)])]
    all_to_all x0 -> x3, waiting for transfers between devices: none -> 5.41 us  [the longest x1 4.37 us: per_device(): parts = lax.all_to_all(parts, 'tensor', 0, 0, tiled=True)]
    ppermute x4 -> x6, starting transfers between devices: 13.7 us -> 17.8 us  [exchange(): lax.ppermute(array, 'replica', [(i, i ^ distance) for i in range(replicas)])]
    pallas_call x3, Pallas kernels: 4.25 us -> 7.88 us  [the longest x1 3.36 us: turn(): pl.pallas_call(shrink_kernel, out_shape=(pltpu.HBM((tensors, slots // 2,...]
    unnamed x16 -> x8, local copies, waits for them, and re-layouts: 3.5 us -> 0.02 us
  transfers between devices with their start and end apart: 4 -> 9, of which waited for: 0 -> 3; matrix products, arithmetic and copies ran while one was open for 0% -> 0% of each run, Pallas kernels for 5% -> 7%
where the time goes in v3:
time: 85.6 us; the launch traced here: 84.2 us
  starting transfers between devices  41.3 us (48%)
  waiting for transfers between devices  15.5 us (18%)
  blocking collectives  14.9 us (17%)
  Pallas kernels  10.8 us (13%)
    ppermute x6, starting transfers between devices, exchange(): lax.ppermute(array, 'replica', [(i, i ^ distance) for i in range(replicas)])  17.8 us
    all_to_all x1, blocking collectives, per_device(): lax.all_to_all(back, 'replica', 0, 0, tiled=True, axis_index_groups=groups)  14.9 us
    all_to_all x1, starting transfers between devices, per_device(): parts = lax.all_to_all(parts, 'tensor', 0, 0, tiled=True)  10.2 us
    ppermute x6, waiting for transfers between devices, exchange(): lax.ppermute(array, 'replica', [(i, i ^ distance) for i in range(replicas)])  10.1 us
    all_to_all x1, starting transfers between devices, per_device(): lax.all_to_all(outgoing, 'replica', 0, 0, tiled=True, axis_index_groups=g...  8.49 us
    all_to_all x1, starting transfers between devices, turn(): low = lax.all_to_all(low, 'tensor', 0, 0, tiled=True)  4.73 us
    all_to_all x1, waiting for transfers between devices, per_device(): parts = lax.all_to_all(parts, 'tensor', 0, 0, tiled=True)  4.37 us
    pallas_call x1, Pallas kernels, turn(): pl.pallas_call(shrink_kernel, out_shape=(pltpu.HBM((tensors, slots // 2,...  3.36 us
  transfers between devices with their start and end apart: 9, of which 3 were waited for; matrix products, arithmetic and copies ran while one was open for 0% of the time, Pallas kernels for 7%

profile of v3, /device:TPU:1, one launch (start us, length us, event | category | flops | bytes accessed | tf_op | source)
XLA Modules:
  0.0 84.2 jit_solution(15376537549256503335)
XLA Ops:
  0.6 0.0 copy-start.3
  0.6 2.6 %attention_part.1 = bf16[16,16,640]{2,1,0:T(8,128)(2,1)} custom-call(s32[4]{0:T(128)} %lengths_hbm.1, bf16[4,4,8192]{2,1,0:T(4,128)(2,1)} %q_hbm.1, bf16[4,4,8,256]{3,2,1,0:T(8,128)(2,1)} %new_hbm.1, bf16[4,8,32,256]{3,2,1,0:T(8,128)(2,1)} %cache_hbm.1), custom_call_target="tpu_custom_call" | custom-call | tf_op jit(solution)/shard_map/attention_part/pallas_call | solution.py:323
  3.3 10.2 %all-to-all-start.1 = ((bf16[16,16,640]{2,1,0:T(8,128)(2,1)}), bf16[16,16,640]{2,1,0:T(8,128)(2,1)S(1)}, u32[]{:S(2)}, u32[]{:S(2)}) async-start(bf16[16,16,640]{2,1,0:T(8,128)(2,1)} %attention_part.1), calls=%async_computation.1 | async-start | bytes 655360 | tf_op jit(solution)/shard_map/all_to_all | solution.py:341
  13.5 0.0 copy-done.3
  13.5 0.1 slice_bitcast_fusion
  13.6 0.0 copy-start
  13.6 0.0 copy-start.1
  13.6 0.0 copy-start.2
  13.6 3.2 %collective-permute-start.2 = (bf16[8,64,512]{2,1,0:T(8,128)(2,1)S(1)}, bf16[8,64,512]{2,1,0:T(8,128)(2,1)S(1)}, u32[]{:S(2)}, u32[]{:S(2)}) collective-permute-start(bf16[8,64,512]{2,1,0:T(8,128)(2,1)S(1)} %get-tuple-element.191.refs_0_), channel_id=1, source_target_pairs={{0,32},{16,48},{32,0},{48,16},{64,96},{80,112},{96,64},{112,80},{1... | collective-permute-start | bytes 1572872 | tf_op jit(solution)/shard_map/ppermute | solution.py:317
  16.9 2.8 %collective-permute-start.1 = (bf16[8,64,512]{2,1,0:T(8,128)(2,1)S(1)}, bf16[8,64,512]{2,1,0:T(8,128)(2,1)S(1)}, u32[]{:S(2)}, u32[]{:S(2)}) collective-permute-start(bf16[8,64,512]{2,1,0:T(8,128)(2,1)S(1)} %get-tuple-element.191.refs_0_), channel_id=1, source_target_pairs={{0,48},{16,32},{32,16},{48,0},{64,112},{80,96},{96,80},{112,64},{1... | collective-permute-start | bytes 1572872 | tf_op jit(solution)/shard_map/ppermute | solution.py:317
  19.6 2.5 %collective-permute-start = (bf16[8,64,512]{2,1,0:T(8,128)(2,1)S(1)}, bf16[8,64,512]{2,1,0:T(8,128)(2,1)S(1)}, u32[]{:S(2)}, u32[]{:S(2)}) collective-permute-start(bf16[8,64,512]{2,1,0:T(8,128)(2,1)S(1)} %get-tuple-element.191.refs_0_), channel_id=1, source_target_pairs={{0,16},{16,0},{32,48},{48,32},{64,80},{80,64},{96,112},{112,96},{1... | collective-permute-start | bytes 1572872 | tf_op jit(solution)/shard_map/ppermute | solution.py:317
  22.2 4.4 %all-to-all-done.1.part_ref = bf16[16,16,640]{2,1,0:T(8,128)(2,1)S(1)} async-done(((bf16[16,16,640]{2,1,0:T(8,128)(2,1)}), bf16[16,16,640]{2,1,0:T(8,128)(2,1)S(1)}, u32[]{:S(2)}, u32[]{:S(2)}) %all-to-all-start.1) | async-done | bytes 327712 | tf_op jit(solution)/shard_map/all_to_all | solution.py:341
  26.5 0.0 copy-done
  26.5 0.0 copy-done.1
  26.5 0.0 copy-done.2
  26.5 2.3 %combine.1 = (bf16[4,4,512]{2,1,0:T(4,128)(2,1)}, bf16[8,16,640]{2,1,0:T(8,128)(2,1)}) custom-call(s32[4]{0:T(128)S(1)} %copy-done, s32[32]{0:T(128)S(1)} %bitcast.13, s32[32]{0:T(128)S(1)} %copy-done.2, bf16[16,16,640]{2,1,0:T(8,128)(2,1)S(1)} %all-to-all-done.1.part_ref), custom_call_target="tpu_custom_call" | custom-call | tf_op jit(solution)/shard_map/combine/pallas_call | solution.py:343
  28.9 8.5 %all-to-all-start.2 = ((bf16[8,16,640]{2,1,0:T(8,128)(2,1)}), bf16[8,16,640]{2,1,0:T(8,128)(2,1)}, u32[]{:S(2)}, u32[]{:S(2)}) async-start(bf16[8,16,640]{2,1,0:T(8,128)(2,1)} %get-tuple-element.75), calls=%async_computation.2 | async-start | bytes 327680 | tf_op jit(solution)/shard_map/all_to_all | solution.py:358
  37.4 4.6 %collective-permute-start.5 = (bf16[8,64,512]{2,1,0:T(8,128)(2,1)S(1)}, bf16[8,64,512]{2,1,0:T(8,128)(2,1)S(1)}, u32[]{:S(2)}, u32[]{:S(2)}) collective-permute-start(bf16[8,64,512]{2,1,0:T(8,128)(2,1)S(1)} %get-tuple-element.195.refs_0_), channel_id=1, source_target_pairs={{0,32},{16,48},{32,0},{48,16},{64,96},{80,112},{96,64},{112,80},{1... | collective-permute-start | bytes 1572872 | tf_op jit(solution)/shard_map/ppermute | solution.py:317
  42.0 2.8 %collective-permute-start.4 = (bf16[8,64,512]{2,1,0:T(8,128)(2,1)S(1)}, bf16[8,64,512]{2,1,0:T(8,128)(2,1)}, u32[]{:S(2)}, u32[]{:S(2)}) collective-permute-start(bf16[8,64,512]{2,1,0:T(8,128)(2,1)S(1)} %get-tuple-element.195.refs_0_), channel_id=1, source_target_pairs={{0,48},{16,32},{32,16},{48,0},{64,112},{80,96},{96,80},{112,64},{1... | collective-permute-start | bytes 1572872 | tf_op jit(solution)/shard_map/ppermute | solution.py:317
  44.8 0.0 collective-permute-done.2.refs_3_
  44.8 1.9 %collective-permute-start.3 = (bf16[8,64,512]{2,1,0:T(8,128)(2,1)S(1)}, bf16[8,64,512]{2,1,0:T(8,128)(2,1)}, u32[]{:S(2)}, u32[]{:S(2)}) collective-permute-start(bf16[8,64,512]{2,1,0:T(8,128)(2,1)S(1)} %get-tuple-element.195.refs_0_), channel_id=1, source_target_pairs={{0,16},{16,0},{32,48},{48,32},{64,80},{80,64},{96,112},{112,96},{1... | collective-permute-start | bytes 1572872 | tf_op jit(solution)/shard_map/ppermute | solution.py:317
  46.8 0.0 collective-permute-done.1.refs_2_
  46.8 0.0 collective-permute-done.refs_1_
  46.8 1.0 %all-to-all-done.2.rows_ref = bf16[8,16,640]{2,1,0:T(8,128)(2,1)} async-done(((bf16[8,16,640]{2,1,0:T(8,128)(2,1)}), bf16[8,16,640]{2,1,0:T(8,128)(2,1)}, u32[]{:S(2)}, u32[]{:S(2)}) %all-to-all-start.2) | async-done | bytes 163872 | tf_op jit(solution)/shard_map/all_to_all | solution.py:358
  47.8 3.4 %shrink_part.2 = (bf16[16,32,128]{2,1,0:T(8,128)(2,1)}, bf16[128,128]{1,0:T(8,128)(2,1)S(1)}, f32[64,128]{1,0:T(8,128)S(1)}, s32[1]{0:T(128)}) custom-call(s32[1]{0:T(128)} %constant.4.clone.1.turn_ref, bf16[8,16,640]{2,1,0:T(8,128)(2,1)} %all-to-all-done.2.rows_ref, bf16[8,64,512]{2,1,0:T(8,128)(2,1)S(1)} %get-tuple-element.191.refs_0_, ...), custom_call_target="tpu_custom_call" | custom-call | tf_op jit(solution)/shard_map/shrink_part/pallas_call | solution.py:365
  51.2 4.7 %all-to-all-start.3 = ((bf16[16,32,128]{2,1,0:T(8,128)(2,1)}), bf16[16,32,128]{2,1,0:T(8,128)(2,1)S(1)}, u32[]{:S(2)}, u32[]{:S(2)}) async-start(bf16[16,32,128]{2,1,0:T(8,128)(2,1)} %get-tuple-element.76), calls=%async_computation.3 | async-start | bytes 262144 | tf_op jit(solution)/shard_map/all_to_all | solution.py:382
  55.9 0.0 collective-permute-done.5.refs_3_
  55.9 10.1 %collective-permute-done.4.refs_2_ = bf16[8,64,512]{2,1,0:T(8,128)(2,1)} collective-permute-done((bf16[8,64,512]{2,1,0:T(8,128)(2,1)S(1)}, bf16[8,64,512]{2,1,0:T(8,128)(2,1)}, u32[]{:S(2)}, u32[]{:S(2)}) %collective-permute-start.4) | collective-permute-done | bytes 524320 | tf_op jit(solution)/shard_map/ppermute | solution.py:317
  66.0 0.0 collective-permute-done.3.refs_1_
  66.0 0.0 all-to-all-done.3.part_ref
  66.0 1.9 %expand_rows.2 = bf16[8,16,512]{2,1,0:T(8,128)(2,1)S(1)} custom-call(bf16[16,32,128]{2,1,0:T(8,128)(2,1)S(1)} %all-to-all-done.3.part_ref, bf16[128,128]{1,0:T(8,128)(2,1)S(1)} %get-tuple-element.77.place_ref, f32[64,128]{1,0:T(8,128)S(1)} %get-tuple-element.78.chosen_ref, bf16[8,64,512]{2,1,0:T(8,128)(2,1)S(1)} %get-tuple-element.195.refs_0_, ...), custom_call_target="tpu_custom_call" | custom-call | tf_op jit(solution)/shard_map/expand_rows/pallas_call | solution.py:383
  67.9 0.7 while.10
  68.6 14.9 %all_to_all.26.part_ref = bf16[8,16,512]{2,1,0:T(8,128)(2,1)S(1)} all-to-all(bf16[8,16,512]{2,1,0:T(8,128)(2,1)S(1)} %get-tuple-element.80), channel_id=1, replica_groups={{0,64,128,192,256,320,384,448},{16,80,144,208,272,336,400,464},{32,96,1..., dimensions={0} | all-to-all | bytes 262144 | tf_op jit(solution)/shard_map/all_to_all | solution.py:399
  83.5 0.6 returned_rows.1
Async XLA Ops:
  0.6 12.9 %copy-start.3 = (bf16[8,2,64,512]{3,2,1,0:T(8,128)(2,1)S(1)}, bf16[8,2,64,512]{3,2,1,0:T(8,128)(2,1)}, u32[]{:S(2)}) copy-start(bf16[8,2,64,512]{3,2,1,0:T(8,128)(2,1)} %param.14) | copy-start | bytes 3145732
  3.3 23.3 %all-to-all-start.1 = ((bf16[16,16,640]{2,1,0:T(8,128)(2,1)}), bf16[16,16,640]{2,1,0:T(8,128)(2,1)S(1)}, u32[]{:S(2)}, u32[]{:S(2)}) async-start(bf16[16,16,640]{2,1,0:T(8,128)(2,1)} %attention_part.1), calls=%async_computation.1 | async-start | bytes 655360 | tf_op jit(solution)/shard_map/all_to_all | solution.py:341
  13.6 12.9 %copy-start = (s32[4]{0:T(128)S(1)}, s32[4]{0:T(128)}, u32[]{:S(2)}) copy-start(s32[4]{0:T(128)} %slots_ref.1) | copy-start | bytes 52
  13.6 12.9 %copy-start.1 = (s32[32,1]{0,1:T(1,128)S(1)}, s32[32,1]{0,1:T(1,128)}, u32[]{:S(2)}) copy-start(s32[32,1]{0,1:T(1,128)} %param.16) | copy-start | bytes 388
  13.6 12.9 %copy-start.2 = (s32[32]{0:T(128)S(1)}, s32[32]{0:T(128)}, u32[]{:S(2)}) copy-start(s32[32]{0:T(128)} %source_slot_ref.1) | copy-start | bytes 388
  13.6 31.2 %collective-permute-start.2 = (bf16[8,64,512]{2,1,0:T(8,128)(2,1)S(1)}, bf16[8,64,512]{2,1,0:T(8,128)(2,1)S(1)}, u32[]{:S(2)}, u32[]{:S(2)}) collective-permute-start(bf16[8,64,512]{2,1,0:T(8,128)(2,1)S(1)} %get-tuple-element.191.refs_0_), channel_id=1, source_target_pairs={{0,32},{16,48},{32,0},{48,16},{64,96},{80,112},{96,64},{112,80},{1... | collective-permute-start | bytes 1572872 | tf_op jit(solution)/shard_map/ppermute | solution.py:317
  16.9 29.9 %collective-permute-start.1 = (bf16[8,64,512]{2,1,0:T(8,128)(2,1)S(1)}, bf16[8,64,512]{2,1,0:T(8,128)(2,1)S(1)}, u32[]{:S(2)}, u32[]{:S(2)}) collective-permute-start(bf16[8,64,512]{2,1,0:T(8,128)(2,1)S(1)} %get-tuple-element.191.refs_0_), channel_id=1, source_target_pairs={{0,48},{16,32},{32,16},{48,0},{64,112},{80,96},{96,80},{112,64},{1... | collective-permute-start | bytes 1572872 | tf_op jit(solution)/shard_map/ppermute | solution.py:317
  19.6 27.1 %collective-permute-start = (bf16[8,64,512]{2,1,0:T(8,128)(2,1)S(1)}, bf16[8,64,512]{2,1,0:T(8,128)(2,1)S(1)}, u32[]{:S(2)}, u32[]{:S(2)}) collective-permute-start(bf16[8,64,512]{2,1,0:T(8,128)(2,1)S(1)} %get-tuple-element.191.refs_0_), channel_id=1, source_target_pairs={{0,16},{16,0},{32,48},{48,32},{64,80},{80,64},{96,112},{112,96},{1... | collective-permute-start | bytes 1572872 | tf_op jit(solution)/shard_map/ppermute | solution.py:317
  28.9 18.9 %all-to-all-start.2 = ((bf16[8,16,640]{2,1,0:T(8,128)(2,1)}), bf16[8,16,640]{2,1,0:T(8,128)(2,1)}, u32[]{:S(2)}, u32[]{:S(2)}) async-start(bf16[8,16,640]{2,1,0:T(8,128)(2,1)} %get-tuple-element.75), calls=%async_computation.2 | async-start | bytes 327680 | tf_op jit(solution)/shard_map/all_to_all | solution.py:358
  37.4 18.5 %collective-permute-start.5 = (bf16[8,64,512]{2,1,0:T(8,128)(2,1)S(1)}, bf16[8,64,512]{2,1,0:T(8,128)(2,1)S(1)}, u32[]{:S(2)}, u32[]{:S(2)}) collective-permute-start(bf16[8,64,512]{2,1,0:T(8,128)(2,1)S(1)} %get-tuple-element.195.refs_0_), channel_id=1, source_target_pairs={{0,32},{16,48},{32,0},{48,16},{64,96},{80,112},{96,64},{112,80},{1... | collective-permute-start | bytes 1572872 | tf_op jit(solution)/shard_map/ppermute | solution.py:317
  42.0 24.0 %collective-permute-start.4 = (bf16[8,64,512]{2,1,0:T(8,128)(2,1)S(1)}, bf16[8,64,512]{2,1,0:T(8,128)(2,1)}, u32[]{:S(2)}, u32[]{:S(2)}) collective-permute-start(bf16[8,64,512]{2,1,0:T(8,128)(2,1)S(1)} %get-tuple-element.195.refs_0_), channel_id=1, source_target_pairs={{0,48},{16,32},{32,16},{48,0},{64,112},{80,96},{96,80},{112,64},{1... | collective-permute-start | bytes 1572872 | tf_op jit(solution)/shard_map/ppermute | solution.py:317
  44.8 21.2 %collective-permute-start.3 = (bf16[8,64,512]{2,1,0:T(8,128)(2,1)S(1)}, bf16[8,64,512]{2,1,0:T(8,128)(2,1)}, u32[]{:S(2)}, u32[]{:S(2)}) collective-permute-start(bf16[8,64,512]{2,1,0:T(8,128)(2,1)S(1)} %get-tuple-element.195.refs_0_), channel_id=1, source_target_pairs={{0,16},{16,0},{32,48},{48,32},{64,80},{80,64},{96,112},{112,96},{1... | collective-permute-start | bytes 1572872 | tf_op jit(solution)/shard_map/ppermute | solution.py:317
  51.2 14.8 %all-to-all-start.3 = ((bf16[16,32,128]{2,1,0:T(8,128)(2,1)}), bf16[16,32,128]{2,1,0:T(8,128)(2,1)S(1)}, u32[]{:S(2)}, u32[]{:S(2)}) async-start(bf16[16,32,128]{2,1,0:T(8,128)(2,1)} %get-tuple-element.76), calls=%async_computation.3 | async-start | bytes 262144 | tf_op jit(solution)/shard_map/all_to_all | solution.py:382

commit v4 on v3

--- a/solution.py
+++ b/solution.py
@@ -14,7 +14,7 @@
 NEG_LARGE = -1e30
 LANES = 128
 LOG2_E = 1.4426950408889634
-BLOCK = (0, 1, 3, 2)
+HELD = (0, 1, 3, X_SIZE)
 ROWS = 4
 AT_ONCE = 16
 
@@ -202,7 +202,7 @@
 
 def page_blocks(refs, at_once):
     replica_here = lax.axis_index("replica")
-    for distance, ref in zip(BLOCK, refs):
+    for distance, ref in zip(HELD, refs):
         first = jnp.bitwise_xor(replica_here, distance) * SLOTS
         for p in range(0, ref.shape[0], at_once):
             block = ref[p : p + at_once]
@@ -215,8 +215,8 @@
     *refs,
 ):
     members, steps_rows, padded = rows_ref.shape
-    page_refs = refs[: len(BLOCK)]
-    out_hbm, place_ref, chosen_ref, count_ref, out_ref, sent = refs[len(BLOCK) :]
+    page_refs = refs[: len(HELD)]
+    out_hbm, place_ref, chosen_ref, count_ref, out_ref, sent = refs[len(HELD) :]
     rank, width = page_refs[0].shape[1:]
     count = members * steps_rows
     rows = ROWS
@@ -224,8 +224,8 @@
     data = rows_ref[...].reshape(count, padded)
     x, page = data[:, :width], data[:, width:].astype(f32)
     distance = jnp.bitwise_xor(page.astype(jnp.int32) // SLOTS, lax.axis_index("replica"))
-    held = distance == BLOCK[0]
-    for other in BLOCK[1:]:
+    held = distance == HELD[0]
+    for other in HELD[1:]:
         held = held | (distance == other)
     held = held.astype(f32)
     one, other = iota((count, count), 0), iota((count, count), 1)
@@ -304,7 +304,9 @@
 ):
     replicas, tensors = lax.axis_size("replica"), lax.axis_size("tensor")
     z_size = replicas // X_SIZE
-    groups = [[z * X_SIZE + x for z in range(z_size)] for x in range(X_SIZE)]
+    groups = [
+        [z * X_SIZE + (x ^ (z % 2 * X_SIZE // 2)) for z in range(z_size)] for x in range(X_SIZE)
+    ]
     members = len(groups[0])
     steps, rows, model = queries.shape
     width = model // tensors
@@ -317,8 +319,8 @@
         return lax.ppermute(array, "replica", [(i, i ^ distance) for i in range(replicas)])
 
     shrink_own, expand_own = adapter_pages[:, 0], adapter_pages[:, 1]
-    shrink_pages = [shrink_own] + [exchange(shrink_own, d) for d in BLOCK[1:]]
-    expand_pages = [expand_own] + [exchange(expand_own, d) for d in BLOCK[1:]]
+    shrink_pages = [shrink_own] + [exchange(shrink_own, d) for d in HELD[1:]]
+    expand_pages = [expand_own] + [exchange(expand_own, d) for d in HELD[1:]]
 
     parts = pl.pallas_call(
         attention_kernel,
@@ -370,7 +372,7 @@
                 jax.ShapeDtypeStruct((slots, LANES), f32),
                 jax.ShapeDtypeStruct((1,), jnp.int32),
             ),
-            in_specs=[smem_spec()] + [vmem_spec()] * (1 + len(BLOCK)),
+            in_specs=[smem_spec()] + [vmem_spec()] * (1 + len(HELD)),
             out_specs=(hbm_spec(), vmem_spec(), vmem_spec(), smem_spec()),
             scratch_shapes=[
                 pltpu.VMEM((slots // 2, LANES), bf16),
@@ -382,8 +384,8 @@
         low = lax.all_to_all(low, "tensor", 0, 0, tiled=True)
         back = pl.pallas_call(
             expand_kernel,
-            out_shape=jax.ShapeDtypeStruct((members, sr, width), bf16),
-            in_specs=[vmem_spec()] * (3 + len(BLOCK)),
+            out_shape=pltpu.VMEM((members, sr, width), bf16),
+            in_specs=[vmem_spec()] * (3 + len(HELD)),
             out_specs=vmem_spec(),
             compiler_params=params(),
             name="expand_rows",

time: 85.6 us -> 84.2 us (0.984)
  starting transfers between devices: 41.3 us -> 43.6 us
  waiting for transfers between devices: 15.5 us -> 13.8 us
    ppermute x6, waiting for transfers between devices: 10.1 us -> 5.97 us  [exchange(): lax.ppermute(array, 'replica', [(i, i ^ distance) for i in range(replicas)])]
    all_to_all x1, waiting for transfers between devices: 0.01 us -> 3.2 us  [turn(): low = lax.all_to_all(low, 'tensor', 0, 0, tiled=True)]
    all_to_all x1, starting transfers between devices: 8.49 us -> 10.9 us  [per_device(): lax.all_to_all(outgoing, 'replica', 0, 0, tiled=True, axis_index_groups=g...]
    pallas_call x1, Pallas kernels: 3.36 us -> 2.45 us  [turn(): pl.pallas_call(shrink_kernel, out_shape=(pltpu.HBM((tensors, slots // 2,...]
  transfers between devices with their start and end apart: 9 -> 9, of which waited for: 3 -> 6; matrix products, arithmetic and copies ran while one was open for 0% -> 0% of each run, Pallas kernels for 7% -> 6%
where the time goes in v4:
time: 84.2 us; the launch traced here: 83.5 us
  starting transfers between devices  43.6 us (52%)
  blocking collectives  14.6 us (17%)
  waiting for transfers between devices  13.8 us (16%)
  Pallas kernels  9.95 us (12%)
    ppermute x6, starting transfers between devices, exchange(): lax.ppermute(array, 'replica', [(i, i ^ distance) for i in range(replicas)])  18.5 us
    all_to_all x1, blocking collectives, per_device(): lax.all_to_all(back, 'replica', 0, 0, tiled=True, axis_index_groups=groups)  14.6 us
    all_to_all x1, starting transfers between devices, per_device(): lax.all_to_all(outgoing, 'replica', 0, 0, tiled=True, axis_index_groups=g...  10.9 us
    all_to_all x1, starting transfers between devices, per_device(): parts = lax.all_to_all(parts, 'tensor', 0, 0, tiled=True)  10.2 us
    ppermute x6, waiting for transfers between devices, exchange(): lax.ppermute(array, 'replica', [(i, i ^ distance) for i in range(replicas)])  5.97 us
    all_to_all x1, waiting for transfers between devices, per_device(): parts = lax.all_to_all(parts, 'tensor', 0, 0, tiled=True)  4 us
    all_to_all x1, starting transfers between devices, turn(): low = lax.all_to_all(low, 'tensor', 0, 0, tiled=True)  3.91 us
    all_to_all x1, waiting for transfers between devices, turn(): low = lax.all_to_all(low, 'tensor', 0, 0, tiled=True)  3.2 us
  transfers between devices with their start and end apart: 9, of which 6 were waited for; matrix products, arithmetic and copies ran while one was open for 0% of the time, Pallas kernels for 6%

profile of v4, /device:TPU:1, one launch (start us, length us, event | category | flops | bytes accessed | tf_op | source)
XLA Modules:
  0.0 83.5 jit_solution(6986648259507258927)
XLA Ops:
  0.6 0.0 copy-start.4
  0.6 2.6 %attention_part.1 = bf16[16,16,640]{2,1,0:T(8,128)(2,1)} custom-call(s32[4]{0:T(128)} %lengths_hbm.1, bf16[4,4,8192]{2,1,0:T(4,128)(2,1)} %q_hbm.1, bf16[4,4,8,256]{3,2,1,0:T(8,128)(2,1)} %new_hbm.1, bf16[4,8,32,256]{3,2,1,0:T(8,128)(2,1)} %cache_hbm.1), custom_call_target="tpu_custom_call" | custom-call | tf_op jit(solution)/shard_map/attention_part/pallas_call | solution.py:325
  3.3 10.2 %all-to-all-start.1 = ((bf16[16,16,640]{2,1,0:T(8,128)(2,1)}), bf16[16,16,640]{2,1,0:T(8,128)(2,1)S(1)}, u32[]{:S(2)}, u32[]{:S(2)}) async-start(bf16[16,16,640]{2,1,0:T(8,128)(2,1)} %attention_part.1), calls=%async_computation.1 | async-start | bytes 655360 | tf_op jit(solution)/shard_map/all_to_all | solution.py:343
  13.5 0.0 copy-done.4
  13.5 0.1 slice_bitcast_fusion
  13.6 0.0 copy-start
  13.6 0.0 copy-start.1
  13.6 0.0 copy-start.2
  13.6 2.6 %collective-permute-start.2 = (bf16[8,64,512]{2,1,0:T(8,128)(2,1)S(1)}, bf16[8,64,512]{2,1,0:T(8,128)(2,1)S(1)}, u32[]{:S(2)}, u32[]{:S(2)}) collective-permute-start(bf16[8,64,512]{2,1,0:T(8,128)(2,1)S(1)} %get-tuple-element.191.refs_0_), channel_id=1, source_target_pairs={{0,64},{16,80},{32,96},{48,112},{64,0},{80,16},{96,32},{112,48},{1... | collective-permute-start | bytes 1572872 | tf_op jit(solution)/shard_map/ppermute | solution.py:319
  16.2 4.4 %collective-permute-start.1 = (bf16[8,64,512]{2,1,0:T(8,128)(2,1)S(1)}, bf16[8,64,512]{2,1,0:T(8,128)(2,1)S(1)}, u32[]{:S(2)}, u32[]{:S(2)}) collective-permute-start(bf16[8,64,512]{2,1,0:T(8,128)(2,1)S(1)} %get-tuple-element.191.refs_0_), channel_id=1, source_target_pairs={{0,48},{16,32},{32,16},{48,0},{64,112},{80,96},{96,80},{112,64},{1... | collective-permute-start | bytes 1572872 | tf_op jit(solution)/shard_map/ppermute | solution.py:319
  20.6 1.9 %collective-permute-start = (bf16[8,64,512]{2,1,0:T(8,128)(2,1)S(1)}, bf16[8,64,512]{2,1,0:T(8,128)(2,1)S(1)}, u32[]{:S(2)}, u32[]{:S(2)}) collective-permute-start(bf16[8,64,512]{2,1,0:T(8,128)(2,1)S(1)} %get-tuple-element.191.refs_0_), channel_id=1, source_target_pairs={{0,16},{16,0},{32,48},{48,32},{64,80},{80,64},{96,112},{112,96},{1... | collective-permute-start | bytes 1572872 | tf_op jit(solution)/shard_map/ppermute | solution.py:319
  22.5 4.0 %all-to-all-done.1.part_ref = bf16[16,16,640]{2,1,0:T(8,128)(2,1)S(1)} async-done(((bf16[16,16,640]{2,1,0:T(8,128)(2,1)}), bf16[16,16,640]{2,1,0:T(8,128)(2,1)S(1)}, u32[]{:S(2)}, u32[]{:S(2)}) %all-to-all-start.1) | async-done | bytes 327712 | tf_op jit(solution)/shard_map/all_to_all | solution.py:343
  26.5 0.0 copy-done
  26.5 0.0 copy-done.1
  26.5 0.0 copy-done.2
  26.6 2.4 %combine.1 = (bf16[4,4,512]{2,1,0:T(4,128)(2,1)}, bf16[8,16,640]{2,1,0:T(8,128)(2,1)}) custom-call(s32[4]{0:T(128)S(1)} %copy-done, s32[32]{0:T(128)S(1)} %bitcast.13, s32[32]{0:T(128)S(1)} %copy-done.2, bf16[16,16,640]{2,1,0:T(8,128)(2,1)S(1)} %all-to-all-done.1.part_ref), custom_call_target="tpu_custom_call" | custom-call | tf_op jit(solution)/shard_map/combine/pallas_call | solution.py:345
  28.9 10.9 %all-to-all-start.2 = ((bf16[8,16,640]{2,1,0:T(8,128)(2,1)}), bf16[8,16,640]{2,1,0:T(8,128)(2,1)S(1)}, u32[]{:S(2)}, u32[]{:S(2)}) async-start(bf16[8,16,640]{2,1,0:T(8,128)(2,1)} %get-tuple-element.75), calls=%async_computation.2 | async-start | bytes 327680 | tf_op jit(solution)/shard_map/all_to_all | solution.py:360
  39.9 3.3 %collective-permute-start.5 = (bf16[8,64,512]{2,1,0:T(8,128)(2,1)S(1)}, bf16[8,64,512]{2,1,0:T(8,128)(2,1)S(1)}, u32[]{:S(2)}, u32[]{:S(2)}) collective-permute-start(bf16[8,64,512]{2,1,0:T(8,128)(2,1)S(1)} %get-tuple-element.195.refs_0_), channel_id=1, source_target_pairs={{0,64},{16,80},{32,96},{48,112},{64,0},{80,16},{96,32},{112,48},{1... | collective-permute-start | bytes 1572872 | tf_op jit(solution)/shard_map/ppermute | solution.py:319
  43.2 4.3 %collective-permute-start.4 = (bf16[8,64,512]{2,1,0:T(8,128)(2,1)S(1)}, bf16[8,64,512]{2,1,0:T(8,128)(2,1)}, u32[]{:S(2)}, u32[]{:S(2)}) collective-permute-start(bf16[8,64,512]{2,1,0:T(8,128)(2,1)S(1)} %get-tuple-element.195.refs_0_), channel_id=1, source_target_pairs={{0,48},{16,32},{32,16},{48,0},{64,112},{80,96},{96,80},{112,64},{1... | collective-permute-start | bytes 1572872 | tf_op jit(solution)/shard_map/ppermute | solution.py:319
  47.6 0.0 collective-permute-done.2.refs_3_
  47.6 1.9 %collective-permute-start.3 = (bf16[8,64,512]{2,1,0:T(8,128)(2,1)S(1)}, bf16[8,64,512]{2,1,0:T(8,128)(2,1)}, u32[]{:S(2)}, u32[]{:S(2)}) collective-permute-start(bf16[8,64,512]{2,1,0:T(8,128)(2,1)S(1)} %get-tuple-element.195.refs_0_), channel_id=1, source_target_pairs={{0,16},{16,0},{32,48},{48,32},{64,80},{80,64},{96,112},{112,96},{1... | collective-permute-start | bytes 1572872 | tf_op jit(solution)/shard_map/ppermute | solution.py:319
  49.5 0.0 collective-permute-done.1.refs_2_
  49.5 0.0 collective-permute-done.refs_1_
  49.5 0.6 all-to-all-done.2.rows_ref
  50.2 0.0 copy-start.3
  50.2 2.4 %shrink_part.2 = (bf16[16,32,128]{2,1,0:T(8,128)(2,1)}, bf16[128,128]{1,0:T(8,128)(2,1)S(1)}, f32[64,128]{1,0:T(8,128)S(1)}, s32[1]{0:T(128)}) custom-call(s32[1]{0:T(128)} %constant.4.clone.1.turn_ref, bf16[8,16,640]{2,1,0:T(8,128)(2,1)S(1)} %all-to-all-done.2.rows_ref, bf16[8,64,512]{2,1,0:T(8,128)(2,1)S(1)} %get-tuple-element.191.refs_0_, ...), custom_call_target="tpu_custom_call" | custom-call | tf_op jit(solution)/shard_map/shrink_part/pallas_call | solution.py:367
  52.6 0.0 copy-done.3
  52.6 3.9 %all-to-all-start.3 = ((bf16[16,32,128]{2,1,0:T(8,128)(2,1)}), bf16[16,32,128]{2,1,0:T(8,128)(2,1)S(1)}, u32[]{:S(2)}, u32[]{:S(2)}) async-start(bf16[16,32,128]{2,1,0:T(8,128)(2,1)} %get-tuple-element.76), calls=%async_computation.3 | async-start | bytes 262144 | tf_op jit(solution)/shard_map/all_to_all | solution.py:384
  56.5 0.9 %collective-permute-done.5.refs_3_ = bf16[8,64,512]{2,1,0:T(8,128)(2,1)S(1)} collective-permute-done((bf16[8,64,512]{2,1,0:T(8,128)(2,1)S(1)}, bf16[8,64,512]{2,1,0:T(8,128)(2,1)S(1)}, u32[]{:S(2)}, u32[]{:S(2)}) %collective-permute-start.5) | collective-permute-done | bytes 524320 | tf_op jit(solution)/shard_map/ppermute | solution.py:319
  57.4 2.9 %collective-permute-done.4.refs_2_ = bf16[8,64,512]{2,1,0:T(8,128)(2,1)} collective-permute-done((bf16[8,64,512]{2,1,0:T(8,128)(2,1)S(1)}, bf16[8,64,512]{2,1,0:T(8,128)(2,1)}, u32[]{:S(2)}, u32[]{:S(2)}) %collective-permute-start.4) | collective-permute-done | bytes 524320 | tf_op jit(solution)/shard_map/ppermute | solution.py:319
  60.3 2.2 %collective-permute-done.3.refs_1_ = bf16[8,64,512]{2,1,0:T(8,128)(2,1)} collective-permute-done((bf16[8,64,512]{2,1,0:T(8,128)(2,1)S(1)}, bf16[8,64,512]{2,1,0:T(8,128)(2,1)}, u32[]{:S(2)}, u32[]{:S(2)}) %collective-permute-start.3) | collective-permute-done | bytes 524320 | tf_op jit(solution)/shard_map/ppermute | solution.py:319
  62.5 3.2 %all-to-all-done.3.part_ref = bf16[16,32,128]{2,1,0:T(8,128)(2,1)S(1)} async-done(((bf16[16,32,128]{2,1,0:T(8,128)(2,1)}), bf16[16,32,128]{2,1,0:T(8,128)(2,1)S(1)}, u32[]{:S(2)}, u32[]{:S(2)}) %all-to-all-start.3) | async-done | bytes 131104 | tf_op jit(solution)/shard_map/all_to_all | solution.py:384
  65.7 1.9 %expand_rows.2 = bf16[8,16,512]{2,1,0:T(8,128)(2,1)S(1)} custom-call(bf16[16,32,128]{2,1,0:T(8,128)(2,1)S(1)} %all-to-all-done.3.part_ref, bf16[128,128]{1,0:T(8,128)(2,1)S(1)} %get-tuple-element.77.place_ref, f32[64,128]{1,0:T(8,128)S(1)} %get-tuple-element.78.chosen_ref, bf16[8,64,512]{2,1,0:T(8,128)(2,1)S(1)} %get-tuple-element.195.refs_0_, ...), custom_call_target="tpu_custom_call" | custom-call | tf_op jit(solution)/shard_map/expand_rows/pallas_call | solution.py:385
  67.6 0.7 while.10
  68.3 14.6 %all_to_all.26.part_ref = bf16[8,16,512]{2,1,0:T(8,128)(2,1)S(1)} all-to-all(bf16[8,16,512]{2,1,0:T(8,128)(2,1)S(1)} %get-tuple-element.80), channel_id=1, replica_groups={{0,96,128,224,256,352,384,480},{16,112,144,240,272,368,400,496},{32,64,..., dimensions={0} | all-to-all | bytes 262144 | tf_op jit(solution)/shard_map/all_to_all | solution.py:401
  82.9 0.6 returned_rows.1
Async XLA Ops:
  0.6 12.9 %copy-start.4 = (bf16[8,2,64,512]{3,2,1,0:T(8,128)(2,1)S(1)}, bf16[8,2,64,512]{3,2,1,0:T(8,128)(2,1)}, u32[]{:S(2)}) copy-start(bf16[8,2,64,512]{3,2,1,0:T(8,128)(2,1)} %param.14) | copy-start | bytes 3145732
  3.3 23.3 %all-to-all-start.1 = ((bf16[16,16,640]{2,1,0:T(8,128)(2,1)}), bf16[16,16,640]{2,1,0:T(8,128)(2,1)S(1)}, u32[]{:S(2)}, u32[]{:S(2)}) async-start(bf16[16,16,640]{2,1,0:T(8,128)(2,1)} %attention_part.1), calls=%async_computation.1 | async-start | bytes 655360 | tf_op jit(solution)/shard_map/all_to_all | solution.py:343
  13.6 12.9 %copy-start = (s32[4]{0:T(128)S(1)}, s32[4]{0:T(128)}, u32[]{:S(2)}) copy-start(s32[4]{0:T(128)} %slots_ref.1) | copy-start | bytes 52
  13.6 12.9 %copy-start.1 = (s32[32,1]{0,1:T(1,128)S(1)}, s32[32,1]{0,1:T(1,128)}, u32[]{:S(2)}) copy-start(s32[32,1]{0,1:T(1,128)} %param.16) | copy-start | bytes 388
  13.6 12.9 %copy-start.2 = (s32[32]{0:T(128)S(1)}, s32[32]{0:T(128)}, u32[]{:S(2)}) copy-start(s32[32]{0:T(128)} %source_slot_ref.1) | copy-start | bytes 388
  13.6 33.9 %collective-permute-start.2 = (bf16[8,64,512]{2,1,0:T(8,128)(2,1)S(1)}, bf16[8,64,512]{2,1,0:T(8,128)(2,1)S(1)}, u32[]{:S(2)}, u32[]{:S(2)}) collective-permute-start(bf16[8,64,512]{2,1,0:T(8,128)(2,1)S(1)} %get-tuple-element.191.refs_0_), channel_id=1, source_target_pairs={{0,64},{16,80},{32,96},{48,112},{64,0},{80,16},{96,32},{112,48},{1... | collective-permute-start | bytes 1572872 | tf_op jit(solution)/shard_map/ppermute | solution.py:319
  16.2 33.3 %collective-permute-start.1 = (bf16[8,64,512]{2,1,0:T(8,128)(2,1)S(1)}, bf16[8,64,512]{2,1,0:T(8,128)(2,1)S(1)}, u32[]{:S(2)}, u32[]{:S(2)}) collective-permute-start(bf16[8,64,512]{2,1,0:T(8,128)(2,1)S(1)} %get-tuple-element.191.refs_0_), channel_id=1, source_target_pairs={{0,48},{16,32},{32,16},{48,0},{64,112},{80,96},{96,80},{112,64},{1... | collective-permute-start | bytes 1572872 | tf_op jit(solution)/shard_map/ppermute | solution.py:319
  20.6 28.9 %collective-permute-start = (bf16[8,64,512]{2,1,0:T(8,128)(2,1)S(1)}, bf16[8,64,512]{2,1,0:T(8,128)(2,1)S(1)}, u32[]{:S(2)}, u32[]{:S(2)}) collective-permute-start(bf16[8,64,512]{2,1,0:T(8,128)(2,1)S(1)} %get-tuple-element.191.refs_0_), channel_id=1, source_target_pairs={{0,16},{16,0},{32,48},{48,32},{64,80},{80,64},{96,112},{112,96},{1... | collective-permute-start | bytes 1572872 | tf_op jit(solution)/shard_map/ppermute | solution.py:319
  28.9 21.3 %all-to-all-start.2 = ((bf16[8,16,640]{2,1,0:T(8,128)(2,1)}), bf16[8,16,640]{2,1,0:T(8,128)(2,1)S(1)}, u32[]{:S(2)}, u32[]{:S(2)}) async-start(bf16[8,16,640]{2,1,0:T(8,128)(2,1)} %get-tuple-element.75), calls=%async_computation.2 | async-start | bytes 327680 | tf_op jit(solution)/shard_map/all_to_all | solution.py:360
  39.9 17.6 %collective-permute-start.5 = (bf16[8,64,512]{2,1,0:T(8,128)(2,1)S(1)}, bf16[8,64,512]{2,1,0:T(8,128)(2,1)S(1)}, u32[]{:S(2)}, u32[]{:S(2)}) collective-permute-start(bf16[8,64,512]{2,1,0:T(8,128)(2,1)S(1)} %get-tuple-element.195.refs_0_), channel_id=1, source_target_pairs={{0,64},{16,80},{32,96},{48,112},{64,0},{80,16},{96,32},{112,48},{1... | collective-permute-start | bytes 1572872 | tf_op jit(solution)/shard_map/ppermute | solution.py:319
  43.2 17.1 %collective-permute-start.4 = (bf16[8,64,512]{2,1,0:T(8,128)(2,1)S(1)}, bf16[8,64,512]{2,1,0:T(8,128)(2,1)}, u32[]{:S(2)}, u32[]{:S(2)}) collective-permute-start(bf16[8,64,512]{2,1,0:T(8,128)(2,1)S(1)} %get-tuple-element.195.refs_0_), channel_id=1, source_target_pairs={{0,48},{16,32},{32,16},{48,0},{64,112},{80,96},{96,80},{112,64},{1... | collective-permute-start | bytes 1572872 | tf_op jit(solution)/shard_map/ppermute | solution.py:319
  47.6 14.9 %collective-permute-start.3 = (bf16[8,64,512]{2,1,0:T(8,128)(2,1)S(1)}, bf16[8,64,512]{2,1,0:T(8,128)(2,1)}, u32[]{:S(2)}, u32[]{:S(2)}) collective-permute-start(bf16[8,64,512]{2,1,0:T(8,128)(2,1)S(1)} %get-tuple-element.195.refs_0_), channel_id=1, source_target_pairs={{0,16},{16,0},{32,48},{48,32},{64,80},{80,64},{96,112},{112,96},{1... | collective-permute-start | bytes 1572872 | tf_op jit(solution)/shard_map/ppermute | solution.py:319
  50.2 2.5 %copy-start.3 = (bf16[8,16,640]{2,1,0:T(8,128)(2,1)}, bf16[8,16,640]{2,1,0:T(8,128)(2,1)S(1)}, u32[]{:S(2)}) copy-start(bf16[8,16,640]{2,1,0:T(8,128)(2,1)S(1)} %all-to-all-done.2.rows_ref) | copy-start | bytes 491524
  52.6 13.1 %all-to-all-start.3 = ((bf16[16,32,128]{2,1,0:T(8,128)(2,1)}), bf16[16,32,128]{2,1,0:T(8,128)(2,1)S(1)}, u32[]{:S(2)}, u32[]{:S(2)}) async-start(bf16[16,32,128]{2,1,0:T(8,128)(2,1)} %get-tuple-element.76), calls=%async_computation.3 | async-start | bytes 262144 | tf_op jit(solution)/shard_map/all_to_all | solution.py:384

commit v5 on v4

--- a/solution.py
+++ b/solution.py
@@ -48,8 +48,15 @@
     q_hbm,
     new_hbm,
     cache_hbm,
+    slots_hbm,
+    source_hbm,
+    source_slot_hbm,
     out_hbm,
+    page_ref,
     lengths_ref,
+    slots_ref,
+    source_ref,
+    source_slot_ref,
     q_ref,
     new_ref,
     cache_ref,
@@ -57,17 +64,23 @@
     out_ref,
     arrived,
     sent,
+    planned,
 ):
     copies = [
         pltpu.make_async_copy(q_hbm, q_ref, arrived.at[0]),
         pltpu.make_async_copy(new_hbm, new_ref, arrived.at[1]),
         pltpu.make_async_copy(lengths_hbm, lengths_ref, arrived.at[2]),
     ]
+    plan_copies = [
+        pltpu.make_async_copy(slots_hbm, slots_ref, planned.at[0]),
+        pltpu.make_async_copy(source_hbm, source_ref, planned.at[1]),
+        pltpu.make_async_copy(source_slot_hbm, source_slot_ref, planned.at[2]),
+    ]
     cache_copies = [
         pltpu.make_async_copy(cache_hbm.at[:, g], cache_ref.at[g], arrived.at[3 + g])
         for g in range(cache_ref.shape[0])
     ]
-    for copy in copies + cache_copies:
+    for copy in copies + cache_copies + plan_copies:
         copy.start()
     steps, rows, width = q_ref.shape
     kv_heads, local = cache_ref.shape[0], cache_ref.shape[2]
@@ -139,38 +152,8 @@
             pltpu.make_async_copy(out_ref.at[here], out_hbm.at[here], sent.at[g])
         )
         out_copies[-1].start()
-    for copy in out_copies:
+    for copy in plan_copies:
         copy.wait()
-
-
-def send_all(ref, hbm, sent):
-    copies = [
-        pltpu.make_async_copy(ref, hbm.at[i], sent.at[i]) for i in range(hbm.shape[0])
-    ]
-    for copy in copies:
-        copy.start()
-    for copy in copies:
-        copy.wait()
-
-
-def combine_kernel(slots_ref, source_ref, source_slot_ref, part_ref, attended_ref, send_hbm, send_ref, sent):
-    steps, rows, width = attended_ref.shape
-    sources = part_ref.shape[0]
-    per_tile = width // LANES
-    field = LANES // 2 // per_tile
-    stats = [part_ref[t, :, width:].astype(f32) for t in range(sources)]
-    top = stats[0]
-    for t in range(1, sources):
-        top = jnp.maximum(top, stats[t])
-    sums = [jnp.zeros((steps * rows, LANES), f32) for _ in range(per_tile)]
-    total = jnp.zeros((steps * rows, LANES), f32)
-    for t in range(sources):
-        fade = jnp.exp2(stats[t] - top)
-        total = total + fade * pltpu.roll(stats[t], LANES // 2, 1)
-        for k in range(per_tile):
-            sums[k] = sums[k] + fade[:, k * field : k * field + 1] * part_ref[
-                t, :, k * LANES : (k + 1) * LANES
-            ].astype(f32)
     replica_here = lax.axis_index("replica")
     row = iota((steps * rows, LANES), 0) % rows
     page = jnp.zeros((steps * rows, LANES), f32)
@@ -183,16 +166,55 @@
             source_ref[entry] * SLOTS + source_slot_ref[entry],
         )
         page = jnp.where(row == r, number.astype(f32), page)
-    page = page.astype(bf16)
+    page_ref[...] = page.astype(bf16)
+    for copy in out_copies:
+        copy.wait()
+
+
+def send_all(ref, hbm, sent):
+    copies = [
+        pltpu.make_async_copy(ref, hbm.at[i], sent.at[i]) for i in range(hbm.shape[0])
+    ]
+    for copy in copies:
+        copy.start()
+    for copy in copies:
+        copy.wait()
+
+
+def combine_kernel(page_ref, part_ref, attended_ref, send_hbm, send_ref, sent):
+    steps, rows, width = attended_ref.shape
+    sources = part_ref.shape[0]
+    per_tile = width // LANES
+    field = LANES // 2 // per_tile
+    sr = steps * rows
+    stats = part_ref[:, :, width:].astype(f32)
+    top = stats[0]
+    for t in range(1, sources):
+        top = jnp.maximum(top, stats[t])
+    fade = jnp.exp2(stats - top[None]).astype(bf16).reshape(sources * sr, LANES)
+    lane, column = iota((LANES, width), 0), iota((LANES, width), 1) // LANES * field
+    spread = lax.dot(fade, (lane == column).astype(f32).astype(bf16), preferred_element_type=f32)
+    totals = lax.dot(
+        part_ref[:, :, width:].reshape(sources * sr, LANES),
+        (lane == column + LANES // 2).astype(f32).astype(bf16),
+        preferred_element_type=f32,
+    )
+    sums = jnp.zeros((sr, width), f32)
+    total = jnp.zeros((sr, width), f32)
+    for t in range(sources):
+        part = slice(t * sr, (t + 1) * sr)
+        sums = sums + spread[part] * part_ref[t, :, :width].astype(f32)
+        total = total + spread[part] * totals[part]
+    attended_all = sums / total
     for k in range(per_tile):
-        attended = sums[k] / total[:, k * field : k * field + 1]
+        attended = attended_all[:, k * LANES : (k + 1) * LANES]
         for s in range(steps):
             attended_ref[s, :, k * LANES : (k + 1) * LANES] = attended[
                 s * rows : (s + 1) * rows
             ].astype(bf16)
         rounded = attended.astype(bf16)
         send_ref[:, k * LANES : (k + 1) * LANES] = rounded
-    send_ref[:, width:] = page
+    send_ref[:, width:] = page_ref[...]
     send_all(send_ref, send_hbm, sent)
 
 
@@ -209,14 +231,12 @@
             yield first + p, block.reshape(at_once * block.shape[1], block.shape[2])
 
 
-def shrink_kernel(
-    turn_ref,
-    rows_ref,
-    *refs,
-):
+def shrink_kernel(rows_ref, *refs):
     members, steps_rows, padded = rows_ref.shape
     page_refs = refs[: len(HELD)]
-    out_hbm, place_ref, chosen_ref, count_ref, out_ref, sent = refs[len(HELD) :]
+    turn_refs = refs[len(HELD) : -5]
+    out_hbm, place_ref, chosen_ref, out_ref, sent = refs[-5:]
+    turn = turn_refs[0][0] if turn_refs else 0
     rank, width = page_refs[0].shape[1:]
     count = members * steps_rows
     rows = ROWS
@@ -237,7 +257,7 @@
     row = iota((count, LANES), 0)
     lane = iota((count, LANES), 1)
     slots = AT_ONCE * steps
-    wanted = turn_ref[0] * AT_ONCE + lane // steps
+    wanted = turn * AT_ONCE + lane // steps
     place = (
         (held > 0.0)
         & (order == wanted.astype(f32))
@@ -245,20 +265,17 @@
         & (lane < slots)
     ).astype(f32).astype(bf16)
     place_ref[...] = place
-    count_ref[0] = jnp.sum(
-        jnp.where((row % steps_rows < rows) & (lane == 0), held, 0.0)
-    ).astype(jnp.int32)
-    down = (((0,), (0,)), ((), ()))
-    x = lax.dot_general(place[:, :slots], x, down, preferred_element_type=f32).astype(bf16)
-    page = lax.dot_general(place[:, :slots], data[:, width:], down, preferred_element_type=f32)
-    chosen_ref[...] = page
     at_once = 256 // rank
-    accum = jnp.zeros((slots, at_once * rank), f32)
+    accum = jnp.zeros((count, at_once * rank), f32)
     for first, block in page_blocks(page_refs, at_once):
         product = lax.dot_general(x, block, (((1,), (1,)), ((), ())), preferred_element_type=f32)
         accum = accum + jnp.where(page_columns(page, first, rank, at_once * rank), product, 0.0)
     folded = accum[:, :LANES] + accum[:, LANES:]
-    folded = folded + pltpu.roll(folded, rank, 1)
+    folded = (folded + pltpu.roll(folded, rank, 1)).astype(bf16)
+    down = (((0,), (0,)), ((), ()))
+    both = jnp.concatenate([folded, data[:, width:]], axis=1)
+    both = lax.dot_general(place[:, :slots], both, down, preferred_element_type=f32)
+    folded, chosen_ref[...] = both[:, :LANES], both[:, LANES:]
     half = slots // 2
     packed = jnp.where(iota((half, LANES), 1) < rank, folded[:half], folded[half:]).astype(bf16)
     out_ref[...] = packed
@@ -322,13 +339,18 @@
     shrink_pages = [shrink_own] + [exchange(shrink_own, d) for d in HELD[1:]]
     expand_pages = [expand_own] + [exchange(expand_own, d) for d in HELD[1:]]
 
-    parts = pl.pallas_call(
+    plan = (request_slots, source_replica[:, 0], source_slot)
+    parts, page = pl.pallas_call(
         attention_kernel,
-        out_shape=pltpu.HBM((tensors, sr, width + LANES), bf16),
-        in_specs=[hbm_spec()] * 4,
-        out_specs=hbm_spec(),
+        out_shape=(
+            pltpu.HBM((tensors, sr, width + LANES), bf16),
+            pltpu.VMEM((sr, LANES), bf16),
+        ),
+        in_specs=[hbm_spec()] * 7,
+        out_specs=(hbm_spec(), vmem_spec()),
         scratch_shapes=[
             pltpu.SMEM(lengths.shape, lengths.dtype),
+            *[pltpu.SMEM(array.shape, array.dtype) for array in plan],
             pltpu.VMEM(queries.shape, bf16),
             pltpu.VMEM(new_entries.shape, bf16),
             pltpu.VMEM((kv_heads,) + cache.shape[:1] + cache.shape[2:], bf16),
@@ -336,10 +358,11 @@
             pltpu.VMEM((tensors, sr, width + LANES), bf16),
             pltpu.SemaphoreType.DMA((3 + kv_heads,)),
             pltpu.SemaphoreType.DMA((kv_heads,)),
+            pltpu.SemaphoreType.DMA((3,)),
         ],
         compiler_params=params(),
         name="attention_part",
-    )(*[in_hbm(array) for array in (lengths, queries, new_entries, cache)])
+    )(*[in_hbm(array) for array in (lengths, queries, new_entries, cache) + plan])
     parts = lax.all_to_all(parts, "tensor", 0, 0, tiled=True)
 
     attended, outgoing = pl.pallas_call(
@@ -348,7 +371,7 @@
             jax.ShapeDtypeStruct((steps, rows, width), bf16),
             pltpu.HBM((members, sr, width + LANES), bf16),
         ),
-        in_specs=[smem_spec(), smem_spec(), smem_spec(), vmem_spec()],
+        in_specs=[vmem_spec(), vmem_spec()],
         out_specs=(vmem_spec(), hbm_spec()),
         scratch_shapes=[
             pltpu.VMEM((sr, width + LANES), bf16),
@@ -356,7 +379,7 @@
         ],
         compiler_params=params(),
         name="combine",
-    )(request_slots, source_replica[:, 0], source_slot, parts)
+    )(page, parts)
     column = lax.all_to_all(
         outgoing, "replica", 0, 0, tiled=True, axis_index_groups=groups
     )
@@ -364,23 +387,23 @@
     slots = AT_ONCE * steps
 
     def turn(k):
-        low, place, chosen, held = pl.pallas_call(
+        number = () if k is None else (jnp.full((1,), k, jnp.int32),)
+        low, place, chosen = pl.pallas_call(
             shrink_kernel,
             out_shape=(
                 pltpu.HBM((tensors, slots // 2, LANES), bf16),
                 jax.ShapeDtypeStruct((count, LANES), bf16),
                 jax.ShapeDtypeStruct((slots, LANES), f32),
-                jax.ShapeDtypeStruct((1,), jnp.int32),
             ),
-            in_specs=[smem_spec()] + [vmem_spec()] * (1 + len(HELD)),
-            out_specs=(hbm_spec(), vmem_spec(), vmem_spec(), smem_spec()),
+            in_specs=[vmem_spec()] * (1 + len(HELD)) + [smem_spec()] * len(number),
+            out_specs=(hbm_spec(), vmem_spec(), vmem_spec()),
             scratch_shapes=[
                 pltpu.VMEM((slots // 2, LANES), bf16),
                 pltpu.SemaphoreType.DMA((tensors,)),
             ],
             compiler_params=params(),
             name="shrink_part",
-        )(jnp.full((1,), k, jnp.int32), column, *shrink_pages)
+        )(column, *shrink_pages, *number)
         low = lax.all_to_all(low, "tensor", 0, 0, tiled=True)
         back = pl.pallas_call(
             expand_kernel,
@@ -390,12 +413,16 @@
             compiler_params=params(),
             name="expand_rows",
         )(low, place, chosen, *expand_pages)
-        return back, held[0]
-
-    back, held = turn(0)
+        return back
+
+    back = turn(None)
+    distance = (column[:, :rows, width].astype(f32).astype(jnp.int32) // SLOTS) ^ lax.axis_index(
+        "replica"
+    )
+    held = sum(jnp.sum((distance == other).astype(jnp.int32)) for other in HELD)
     _, back = lax.while_loop(
         lambda state: state[0] * AT_ONCE < held,
-        lambda state: (state[0] + 1, state[1] + turn(state[0])[0]),
+        lambda state: (state[0] + 1, state[1] + turn(state[0])),
         (jnp.int32(1), back),
     )
     back = lax.all_to_all(back, "replica", 0, 0, tiled=True, axis_index_groups=groups)

time: 84.2 us -> 83.2 us (0.988)
  waiting for transfers between devices: 13.8 us -> 10.1 us
  between operations: 0.8 us -> 3.15 us
  other arithmetic: 0 us -> 1.48 us
  Pallas kernels: 9.95 us -> 8.73 us
  blocking collectives: 14.6 us -> 15.5 us
    ppermute x6, waiting for transfers between devices: 5.97 us -> 2.66 us  [exchange(): lax.ppermute(array, 'replica', [(i, i ^ distance) for i in range(replicas)])]
    all_to_all x1, blocking collectives: 14.6 us -> 15.5 us  [per_device(): lax.all_to_all(back, 'replica', 0, 0, tiled=True, axis_index_groups=groups)]
  transfers between devices with their start and end apart: 9 -> 9, of which waited for: 6 -> 5; matrix products, arithmetic and copies ran while one was open for 0% -> 2% of each run, Pallas kernels for 6% -> 4%
where the time goes in v5:
time: 83.2 us; the launch traced here: 82.5 us
  starting transfers between devices  43.4 us (52%)
  blocking collectives  15.5 us (19%)
  waiting for transfers between devices  10.1 us (12%)
  Pallas kernels  8.73 us (10%)
  between operations  3.15 us (4%)
  other arithmetic  1.48 us (2%)
    ppermute x6, starting transfers between devices, exchange(): lax.ppermute(array, 'replica', [(i, i ^ distance) for i in range(replicas)])  18.4 us
    all_to_all x1, blocking collectives, per_device(): lax.all_to_all(back, 'replica', 0, 0, tiled=True, axis_index_groups=groups)  15.5 us
    all_to_all x1, starting transfers between devices, per_device(): lax.all_to_all(outgoing, 'replica', 0, 0, tiled=True, axis_index_groups=g...  10.9 us
    all_to_all x1, starting transfers between devices, per_device(): parts = lax.all_to_all(parts, 'tensor', 0, 0, tiled=True)  10.2 us
    all_to_all x1, waiting for transfers between devices, per_device(): parts = lax.all_to_all(parts, 'tensor', 0, 0, tiled=True)  4.17 us
    all_to_all x1, starting transfers between devices, turn(): low = lax.all_to_all(low, 'tensor', 0, 0, tiled=True)  3.83 us
    ppermute x6, waiting for transfers between devices, exchange(): lax.ppermute(array, 'replica', [(i, i ^ distance) for i in range(replicas)])  2.66 us
    pallas_call x1, Pallas kernels, per_device(): pl.pallas_call(attention_kernel, out_shape=(pltpu.HBM((tensors, sr, width...  2.66 us
  transfers between devices with their start and end apart: 9, of which 5 were waited for; matrix products, arithmetic and copies ran while one was open for 2% of the time, Pallas kernels for 4%

profile of v5, /device:TPU:1, one launch (start us, length us, event | category | flops | bytes accessed | tf_op | source)
XLA Modules:
  0.0 82.5 jit_solution(10402658567047357953)
XLA Ops:
  0.6 0.0 copy-start.1
  0.6 2.7 %attention_part.1 = (bf16[16,16,640]{2,1,0:T(8,128)(2,1)}, bf16[16,128]{1,0:T(8,128)(2,1)S(1)}) custom-call(s32[4]{0:T(128)} %lengths_hbm.1, bf16[4,4,8192]{2,1,0:T(4,128)(2,1)} %q_hbm.1, bf16[4,4,8,256]{3,2,1,0:T(8,128)(2,1)} %new_hbm.1, bf16[4,8,32,256]{3,2,1,0:T(8,128)(2,1)} %cache_hbm.1, s32[4]{0:T(128)} %slots_hbm.1, s32[32]{0:T(128)} %bitcast.28, ...), custom_call_target="tpu_custom_call" | custom-call | tf_op jit(solution)/shard_map/attention_part/pallas_call | solution.py:343
  3.3 10.2 %all-to-all-start.1 = ((bf16[16,16,640]{2,1,0:T(8,128)(2,1)}), bf16[16,16,640]{2,1,0:T(8,128)(2,1)S(1)}, u32[]{:S(2)}, u32[]{:S(2)}) async-start(bf16[16,16,640]{2,1,0:T(8,128)(2,1)} %get-tuple-element.76), calls=%async_computation.1 | async-start | bytes 655360 | tf_op jit(solution)/shard_map/all_to_all | solution.py:366
  13.5 0.0 copy-done.1
  13.5 0.1 slice_bitcast_fusion
  13.6 2.4 %collective-permute-start.2 = (bf16[8,64,512]{2,1,0:T(8,128)(2,1)S(1)}, bf16[8,64,512]{2,1,0:T(8,128)(2,1)S(1)}, u32[]{:S(2)}, u32[]{:S(2)}) collective-permute-start(bf16[8,64,512]{2,1,0:T(8,128)(2,1)S(1)} %get-tuple-element.197.refs_0_), channel_id=1, source_target_pairs={{0,64},{16,80},{32,96},{48,112},{64,0},{80,16},{96,32},{112,48},{1... | collective-permute-start | bytes 1572872 | tf_op jit(solution)/shard_map/ppermute | solution.py:336
  16.1 4.4 %collective-permute-start.1 = (bf16[8,64,512]{2,1,0:T(8,128)(2,1)S(1)}, bf16[8,64,512]{2,1,0:T(8,128)(2,1)S(1)}, u32[]{:S(2)}, u32[]{:S(2)}) collective-permute-start(bf16[8,64,512]{2,1,0:T(8,128)(2,1)S(1)} %get-tuple-element.197.refs_0_), channel_id=1, source_target_pairs={{0,48},{16,32},{32,16},{48,0},{64,112},{80,96},{96,80},{112,64},{1... | collective-permute-start | bytes 1572872 | tf_op jit(solution)/shard_map/ppermute | solution.py:336
  20.5 1.9 %collective-permute-start = (bf16[8,64,512]{2,1,0:T(8,128)(2,1)S(1)}, bf16[8,64,512]{2,1,0:T(8,128)(2,1)S(1)}, u32[]{:S(2)}, u32[]{:S(2)}) collective-permute-start(bf16[8,64,512]{2,1,0:T(8,128)(2,1)S(1)} %get-tuple-element.197.refs_0_), channel_id=1, source_target_pairs={{0,16},{16,0},{32,48},{48,32},{64,80},{80,64},{96,112},{112,96},{1... | collective-permute-start | bytes 1572872 | tf_op jit(solution)/shard_map/ppermute | solution.py:336
  22.4 4.2 %all-to-all-done.1.part_ref = bf16[16,16,640]{2,1,0:T(8,128)(2,1)S(1)} async-done(((bf16[16,16,640]{2,1,0:T(8,128)(2,1)}), bf16[16,16,640]{2,1,0:T(8,128)(2,1)S(1)}, u32[]{:S(2)}, u32[]{:S(2)}) %all-to-all-start.1) | async-done | bytes 327712 | tf_op jit(solution)/shard_map/all_to_all | solution.py:366
  26.6 1.7 %combine.1 = (bf16[4,4,512]{2,1,0:T(4,128)(2,1)}, bf16[8,16,640]{2,1,0:T(8,128)(2,1)}) custom-call(bf16[16,128]{1,0:T(8,128)(2,1)S(1)} %get-tuple-element.75.page_ref, bf16[16,16,640]{2,1,0:T(8,128)(2,1)S(1)} %all-to-all-done.1.part_ref), custom_call_target="tpu_custom_call" | custom-call | tf_op jit(solution)/shard_map/combine/pallas_call | solution.py:368
  28.2 10.9 %all-to-all-start.2 = ((bf16[8,16,640]{2,1,0:T(8,128)(2,1)}), bf16[8,16,640]{2,1,0:T(8,128)(2,1)S(1)}, u32[]{:S(2)}, u32[]{:S(2)}) async-start(bf16[8,16,640]{2,1,0:T(8,128)(2,1)} %get-tuple-element.78), calls=%async_computation.2 | async-start | bytes 327680 | tf_op jit(solution)/shard_map/all_to_all | solution.py:383
  39.2 3.4 %collective-permute-start.5 = (bf16[8,64,512]{2,1,0:T(8,128)(2,1)S(1)}, bf16[8,64,512]{2,1,0:T(8,128)(2,1)S(1)}, u32[]{:S(2)}, u32[]{:S(2)}) collective-permute-start(bf16[8,64,512]{2,1,0:T(8,128)(2,1)S(1)} %get-tuple-element.201.refs_0_), channel_id=1, source_target_pairs={{0,64},{16,80},{32,96},{48,112},{64,0},{80,16},{96,32},{112,48},{1... | collective-permute-start | bytes 1572872 | tf_op jit(solution)/shard_map/ppermute | solution.py:336
  42.5 4.3 %collective-permute-start.4 = (bf16[8,64,512]{2,1,0:T(8,128)(2,1)S(1)}, bf16[8,64,512]{2,1,0:T(8,128)(2,1)}, u32[]{:S(2)}, u32[]{:S(2)}) collective-permute-start(bf16[8,64,512]{2,1,0:T(8,128)(2,1)S(1)} %get-tuple-element.201.refs_0_), channel_id=1, source_target_pairs={{0,48},{16,32},{32,16},{48,0},{64,112},{80,96},{96,80},{112,64},{1... | collective-permute-start | bytes 1572872 | tf_op jit(solution)/shard_map/ppermute | solution.py:336
  46.9 0.0 collective-permute-done.2.refs_3_
  46.9 1.9 %collective-permute-start.3 = (bf16[8,64,512]{2,1,0:T(8,128)(2,1)S(1)}, bf16[8,64,512]{2,1,0:T(8,128)(2,1)}, u32[]{:S(2)}, u32[]{:S(2)}) collective-permute-start(bf16[8,64,512]{2,1,0:T(8,128)(2,1)S(1)} %get-tuple-element.201.refs_0_), channel_id=1, source_target_pairs={{0,16},{16,0},{32,48},{48,32},{64,80},{80,64},{96,112},{112,96},{1... | collective-permute-start | bytes 1572872 | tf_op jit(solution)/shard_map/ppermute | solution.py:336
  48.8 0.0 collective-permute-done.1.refs_2_
  48.9 0.0 collective-permute-done.refs_1_
  48.9 0.6 all-to-all-done.2.rows_ref
  49.5 0.0 copy-start
  49.5 1.9 %shrink_part.2 = (bf16[16,32,128]{2,1,0:T(8,128)(2,1)}, bf16[128,128]{1,0:T(8,128)(2,1)S(1)}, f32[64,128]{1,0:T(8,128)S(1)}) custom-call(bf16[8,16,640]{2,1,0:T(8,128)(2,1)S(1)} %all-to-all-done.2.rows_ref, bf16[8,64,512]{2,1,0:T(8,128)(2,1)S(1)} %get-tuple-element.197.refs_0_, bf16[8,64,512]{2,1,0:T(8,128)(2,1)S(1)} %collective-permute-done.refs_1_, ...), custom_call_target="tpu_custom_call" | custom-call | tf_op jit(solution)/shard_map/shrink_part/pallas_call | solution.py:391
  51.4 0.0 copy-done
  51.4 3.8 %all-to-all-start.3 = ((bf16[16,32,128]{2,1,0:T(8,128)(2,1)}), bf16[16,32,128]{2,1,0:T(8,128)(2,1)S(1)}, u32[]{:S(2)}, u32[]{:S(2)}) async-start(bf16[16,32,128]{2,1,0:T(8,128)(2,1)} %get-tuple-element.79), calls=%async_computation.3 | async-start | bytes 262144 | tf_op jit(solution)/shard_map/all_to_all | solution.py:407
  55.2 0.7 convert_convert_fusion
  56.0 0.1 copy.15
  56.1 0.8 convert_reduce_fusion
  59.2 0.0 collective-permute-done.5.refs_3_
  59.2 0.5 collective-permute-done.4.refs_2_
  59.7 2.2 %collective-permute-done.3.refs_1_ = bf16[8,64,512]{2,1,0:T(8,128)(2,1)} collective-permute-done((bf16[8,64,512]{2,1,0:T(8,128)(2,1)S(1)}, bf16[8,64,512]{2,1,0:T(8,128)(2,1)}, u32[]{:S(2)}, u32[]{:S(2)}) %collective-permute-start.3) | collective-permute-done | bytes 524320 | tf_op jit(solution)/shard_map/ppermute | solution.py:336
  61.8 2.6 %all-to-all-done.3.part_ref = bf16[16,32,128]{2,1,0:T(8,128)(2,1)S(1)} async-done(((bf16[16,32,128]{2,1,0:T(8,128)(2,1)}), bf16[16,32,128]{2,1,0:T(8,128)(2,1)S(1)}, u32[]{:S(2)}, u32[]{:S(2)}) %all-to-all-start.3) | async-done | bytes 131104 | tf_op jit(solution)/shard_map/all_to_all | solution.py:407
  64.5 1.9 %expand_rows.2 = bf16[8,16,512]{2,1,0:T(8,128)(2,1)S(1)} custom-call(bf16[16,32,128]{2,1,0:T(8,128)(2,1)S(1)} %all-to-all-done.3.part_ref, bf16[128,128]{1,0:T(8,128)(2,1)S(1)} %get-tuple-element.80.place_ref, f32[64,128]{1,0:T(8,128)S(1)} %get-tuple-element.81.chosen_ref, bf16[8,64,512]{2,1,0:T(8,128)(2,1)S(1)} %get-tuple-element.201.refs_0_, ...), custom_call_target="tpu_custom_call" | custom-call | tf_op jit(solution)/shard_map/expand_rows/pallas_call | solution.py:408
  66.4 15.5 %all_to_all.26.part_ref = bf16[8,16,512]{2,1,0:T(8,128)(2,1)S(1)} all-to-all(bf16[8,16,512]{2,1,0:T(8,128)(2,1)S(1)} %get-tuple-element.82), channel_id=1, replica_groups={{0,96,128,224,256,352,384,480},{16,112,144,240,272,368,400,496},{32,64,..., dimensions={0} | all-to-all | bytes 262144 | tf_op jit(solution)/shard_map/all_to_all | solution.py:428
  81.9 0.6 returned_rows.1
  (1 shorter events, 0.0 us)
Async XLA Ops:
  0.6 12.9 %copy-start.1 = (bf16[8,2,64,512]{3,2,1,0:T(8,128)(2,1)S(1)}, bf16[8,2,64,512]{3,2,1,0:T(8,128)(2,1)}, u32[]{:S(2)}) copy-start(bf16[8,2,64,512]{3,2,1,0:T(8,128)(2,1)} %param.14) | copy-start | bytes 3145732
  3.3 23.3 %all-to-all-start.1 = ((bf16[16,16,640]{2,1,0:T(8,128)(2,1)}), bf16[16,16,640]{2,1,0:T(8,128)(2,1)S(1)}, u32[]{:S(2)}, u32[]{:S(2)}) async-start(bf16[16,16,640]{2,1,0:T(8,128)(2,1)} %get-tuple-element.76), calls=%async_computation.1 | async-start | bytes 655360 | tf_op jit(solution)/shard_map/all_to_all | solution.py:366
  13.6 33.3 %collective-permute-start.2 = (bf16[8,64,512]{2,1,0:T(8,128)(2,1)S(1)}, bf16[8,64,512]{2,1,0:T(8,128)(2,1)S(1)}, u32[]{:S(2)}, u32[]{:S(2)}) collective-permute-start(bf16[8,64,512]{2,1,0:T(8,128)(2,1)S(1)} %get-tuple-element.197.refs_0_), channel_id=1, source_target_pairs={{0,64},{16,80},{32,96},{48,112},{64,0},{80,16},{96,32},{112,48},{1... | collective-permute-start | bytes 1572872 | tf_op jit(solution)/shard_map/ppermute | solution.py:336
  16.1 32.8 %collective-permute-start.1 = (bf16[8,64,512]{2,1,0:T(8,128)(2,1)S(1)}, bf16[8,64,512]{2,1,0:T(8,128)(2,1)S(1)}, u32[]{:S(2)}, u32[]{:S(2)}) collective-permute-start(bf16[8,64,512]{2,1,0:T(8,128)(2,1)S(1)} %get-tuple-element.197.refs_0_), channel_id=1, source_target_pairs={{0,48},{16,32},{32,16},{48,0},{64,112},{80,96},{96,80},{112,64},{1... | collective-permute-start | bytes 1572872 | tf_op jit(solution)/shard_map/ppermute | solution.py:336
  20.5 28.4 %collective-permute-start = (bf16[8,64,512]{2,1,0:T(8,128)(2,1)S(1)}, bf16[8,64,512]{2,1,0:T(8,128)(2,1)S(1)}, u32[]{:S(2)}, u32[]{:S(2)}) collective-permute-start(bf16[8,64,512]{2,1,0:T(8,128)(2,1)S(1)} %get-tuple-element.197.refs_0_), channel_id=1, source_target_pairs={{0,16},{16,0},{32,48},{48,32},{64,80},{80,64},{96,112},{112,96},{1... | collective-permute-start | bytes 1572872 | tf_op jit(solution)/shard_map/ppermute | solution.py:336
  28.2 21.3 %all-to-all-start.2 = ((bf16[8,16,640]{2,1,0:T(8,128)(2,1)}), bf16[8,16,640]{2,1,0:T(8,128)(2,1)S(1)}, u32[]{:S(2)}, u32[]{:S(2)}) async-start(bf16[8,16,640]{2,1,0:T(8,128)(2,1)} %get-tuple-element.78), calls=%async_computation.2 | async-start | bytes 327680 | tf_op jit(solution)/shard_map/all_to_all | solution.py:383
  39.2 20.0 %collective-permute-start.5 = (bf16[8,64,512]{2,1,0:T(8,128)(2,1)S(1)}, bf16[8,64,512]{2,1,0:T(8,128)(2,1)S(1)}, u32[]{:S(2)}, u32[]{:S(2)}) collective-permute-start(bf16[8,64,512]{2,1,0:T(8,128)(2,1)S(1)} %get-tuple-element.201.refs_0_), channel_id=1, source_target_pairs={{0,64},{16,80},{32,96},{48,112},{64,0},{80,16},{96,32},{112,48},{1... | collective-permute-start | bytes 1572872 | tf_op jit(solution)/shard_map/ppermute | solution.py:336
  42.5 17.1 %collective-permute-start.4 = (bf16[8,64,512]{2,1,0:T(8,128)(2,1)S(1)}, bf16[8,64,512]{2,1,0:T(8,128)(2,1)}, u32[]{:S(2)}, u32[]{:S(2)}) collective-permute-start(bf16[8,64,512]{2,1,0:T(8,128)(2,1)S(1)} %get-tuple-element.201.refs_0_), channel_id=1, source_target_pairs={{0,48},{16,32},{32,16},{48,0},{64,112},{80,96},{96,80},{112,64},{1... | collective-permute-start | bytes 1572872 | tf_op jit(solution)/shard_map/ppermute | solution.py:336
  46.9 14.9 %collective-permute-start.3 = (bf16[8,64,512]{2,1,0:T(8,128)(2,1)S(1)}, bf16[8,64,512]{2,1,0:T(8,128)(2,1)}, u32[]{:S(2)}, u32[]{:S(2)}) collective-permute-start(bf16[8,64,512]{2,1,0:T(8,128)(2,1)S(1)} %get-tuple-element.201.refs_0_), channel_id=1, source_target_pairs={{0,16},{16,0},{32,48},{48,32},{64,80},{80,64},{96,112},{112,96},{1... | collective-permute-start | bytes 1572872 | tf_op jit(solution)/shard_map/ppermute | solution.py:336
  49.5 1.9 %copy-start = (bf16[8,16,640]{2,1,0:T(8,128)(2,1)}, bf16[8,16,640]{2,1,0:T(8,128)(2,1)S(1)}, u32[]{:S(2)}) copy-start(bf16[8,16,640]{2,1,0:T(8,128)(2,1)S(1)} %all-to-all-done.2.rows_ref) | copy-start | bytes 491524
  51.4 13.0 %all-to-all-start.3 = ((bf16[16,32,128]{2,1,0:T(8,128)(2,1)}), bf16[16,32,128]{2,1,0:T(8,128)(2,1)S(1)}, u32[]{:S(2)}, u32[]{:S(2)}) async-start(bf16[16,32,128]{2,1,0:T(8,128)(2,1)} %get-tuple-element.79), calls=%async_computation.3 | async-start | bytes 262144 | tf_op jit(solution)/shard_map/all_to_all | solution.py:407

commit v6 on v5

--- a/solution.py
+++ b/solution.py
@@ -29,6 +29,10 @@
 
 def in_hbm(array):
     return pltpu.with_memory_space_constraint(array, pltpu.HBM)
+
+
+def in_vmem(array):
+    return pltpu.with_memory_space_constraint(array, pltpu.VMEM)
 
 
 def smem_spec():
@@ -337,7 +341,7 @@
 
     shrink_own, expand_own = adapter_pages[:, 0], adapter_pages[:, 1]
     shrink_pages = [shrink_own] + [exchange(shrink_own, d) for d in HELD[1:]]
-    expand_pages = [expand_own] + [exchange(expand_own, d) for d in HELD[1:]]
+    expand_pages = [expand_own] + [in_vmem(exchange(expand_own, d)) for d in HELD[1:]]
 
     plan = (request_slots, source_replica[:, 0], source_slot)
     parts, page = pl.pallas_call(

time: 83.2 us -> 83.3 us (level)
    ppermute x6, waiting for transfers between devices: 2.66 us -> 1.28 us  [exchange(): lax.ppermute(array, 'replica', [(i, i ^ distance) for i in range(replicas)])]
    all_to_all x1, waiting for transfers between devices: 2.6 us -> 3.98 us  [turn(): low = lax.all_to_all(low, 'tensor', 0, 0, tiled=True)]
    pallas_call x1, Pallas kernels: 1.89 us -> 3.16 us  [turn(): pl.pallas_call(shrink_kernel, out_shape=(pltpu.HBM((tensors, slots // 2,...]
    pallas_call x1, Pallas kernels: 1.89 us -> 0.69 us  [turn(): pl.pallas_call(expand_kernel, out_shape=pltpu.VMEM((members, sr, width),...]
  transfers between devices with their start and end apart: 9 -> 9, of which waited for: 5 -> 4; matrix products, arithmetic and copies ran while one was open for 2% -> 2% of each run, Pallas kernels for 4% -> 6%
where the time goes in v6:
time: 83.3 us; the launch traced here: 82.6 us
  starting transfers between devices  43.3 us (52%)
  blocking collectives  15.5 us (19%)
  waiting for transfers between devices  10.1 us (12%)
  Pallas kernels  8.81 us (11%)
  between operations  3.16 us (4%)
  other arithmetic  1.48 us (2%)
    ppermute x6, starting transfers between devices, exchange(): lax.ppermute(array, 'replica', [(i, i ^ distance) for i in range(replicas)])  18.4 us
    all_to_all x1, blocking collectives, per_device(): lax.all_to_all(back, 'replica', 0, 0, tiled=True, axis_index_groups=groups)  15.5 us
    all_to_all x1, starting transfers between devices, per_device(): lax.all_to_all(outgoing, 'replica', 0, 0, tiled=True, axis_index_groups=g...  10.9 us
    all_to_all x1, starting transfers between devices, per_device(): parts = lax.all_to_all(parts, 'tensor', 0, 0, tiled=True)  10.2 us
    all_to_all x1, waiting for transfers between devices, per_device(): parts = lax.all_to_all(parts, 'tensor', 0, 0, tiled=True)  4.19 us
    all_to_all x1, waiting for transfers between devices, turn(): low = lax.all_to_all(low, 'tensor', 0, 0, tiled=True)  3.98 us
    all_to_all x1, starting transfers between devices, turn(): low = lax.all_to_all(low, 'tensor', 0, 0, tiled=True)  3.82 us
    pallas_call x1, Pallas kernels, turn(): pl.pallas_call(shrink_kernel, out_shape=(pltpu.HBM((tensors, slots // 2,...  3.16 us
  transfers between devices with their start and end apart: 9, of which 4 were waited for; matrix products, arithmetic and copies ran while one was open for 2% of the time, Pallas kernels for 6%

profile of v6, /device:TPU:1, one launch (start us, length us, event | category | flops | bytes accessed | tf_op | source)
XLA Modules:
  0.0 82.6 jit_solution(2580326504103528963)
XLA Ops:
  0.6 0.0 copy-start.1
  0.6 2.7 %attention_part.1 = (bf16[16,16,640]{2,1,0:T(8,128)(2,1)}, bf16[16,128]{1,0:T(8,128)(2,1)S(1)}) custom-call(s32[4]{0:T(128)} %lengths_hbm.1, bf16[4,4,8192]{2,1,0:T(4,128)(2,1)} %q_hbm.1, bf16[4,4,8,256]{3,2,1,0:T(8,128)(2,1)} %new_hbm.1, bf16[4,8,32,256]{3,2,1,0:T(8,128)(2,1)} %cache_hbm.1, s32[4]{0:T(128)} %slots_hbm.1, s32[32]{0:T(128)} %bitcast.28, ...), custom_call_target="tpu_custom_call" | custom-call | tf_op jit(solution)/shard_map/attention_part/pallas_call | solution.py:347
  3.3 10.2 %all-to-all-start.1 = ((bf16[16,16,640]{2,1,0:T(8,128)(2,1)}), bf16[16,16,640]{2,1,0:T(8,128)(2,1)S(1)}, u32[]{:S(2)}, u32[]{:S(2)}) async-start(bf16[16,16,640]{2,1,0:T(8,128)(2,1)} %get-tuple-element.76), calls=%async_computation.1 | async-start | bytes 655360 | tf_op jit(solution)/shard_map/all_to_all | solution.py:370
  13.5 0.0 copy-done.1
  13.5 0.1 slice_bitcast_fusion
  13.6 2.4 %collective-permute-start.2 = (bf16[8,64,512]{2,1,0:T(8,128)(2,1)S(1)}, bf16[8,64,512]{2,1,0:T(8,128)(2,1)S(1)}, u32[]{:S(2)}, u32[]{:S(2)}) collective-permute-start(bf16[8,64,512]{2,1,0:T(8,128)(2,1)S(1)} %get-tuple-element.197.refs_0_), channel_id=1, source_target_pairs={{0,64},{16,80},{32,96},{48,112},{64,0},{80,16},{96,32},{112,48},{1... | collective-permute-start | bytes 1572872 | tf_op jit(solution)/shard_map/ppermute | solution.py:340
  16.1 4.4 %collective-permute-start.1 = (bf16[8,64,512]{2,1,0:T(8,128)(2,1)S(1)}, bf16[8,64,512]{2,1,0:T(8,128)(2,1)}, u32[]{:S(2)}, u32[]{:S(2)}) collective-permute-start(bf16[8,64,512]{2,1,0:T(8,128)(2,1)S(1)} %get-tuple-element.197.refs_0_), channel_id=1, source_target_pairs={{0,48},{16,32},{32,16},{48,0},{64,112},{80,96},{96,80},{112,64},{1... | collective-permute-start | bytes 1572872 | tf_op jit(solution)/shard_map/ppermute | solution.py:340
  20.5 1.9 %collective-permute-start = (bf16[8,64,512]{2,1,0:T(8,128)(2,1)S(1)}, bf16[8,64,512]{2,1,0:T(8,128)(2,1)}, u32[]{:S(2)}, u32[]{:S(2)}) collective-permute-start(bf16[8,64,512]{2,1,0:T(8,128)(2,1)S(1)} %get-tuple-element.197.refs_0_), channel_id=1, source_target_pairs={{0,16},{16,0},{32,48},{48,32},{64,80},{80,64},{96,112},{112,96},{1... | collective-permute-start | bytes 1572872 | tf_op jit(solution)/shard_map/ppermute | solution.py:340
  22.4 4.2 %all-to-all-done.1.part_ref = bf16[16,16,640]{2,1,0:T(8,128)(2,1)S(1)} async-done(((bf16[16,16,640]{2,1,0:T(8,128)(2,1)}), bf16[16,16,640]{2,1,0:T(8,128)(2,1)S(1)}, u32[]{:S(2)}, u32[]{:S(2)}) %all-to-all-start.1) | async-done | bytes 327712 | tf_op jit(solution)/shard_map/all_to_all | solution.py:370
  26.6 1.7 %combine.1 = (bf16[4,4,512]{2,1,0:T(4,128)(2,1)}, bf16[8,16,640]{2,1,0:T(8,128)(2,1)}) custom-call(bf16[16,128]{1,0:T(8,128)(2,1)S(1)} %get-tuple-element.75.page_ref, bf16[16,16,640]{2,1,0:T(8,128)(2,1)S(1)} %all-to-all-done.1.part_ref), custom_call_target="tpu_custom_call" | custom-call | tf_op jit(solution)/shard_map/combine/pallas_call | solution.py:372
  28.2 10.9 %all-to-all-start.2 = ((bf16[8,16,640]{2,1,0:T(8,128)(2,1)}), bf16[8,16,640]{2,1,0:T(8,128)(2,1)S(1)}, u32[]{:S(2)}, u32[]{:S(2)}) async-start(bf16[8,16,640]{2,1,0:T(8,128)(2,1)} %get-tuple-element.78), calls=%async_computation.2 | async-start | bytes 327680 | tf_op jit(solution)/shard_map/all_to_all | solution.py:387
  39.2 3.3 %collective-permute-start.5 = (bf16[8,64,512]{2,1,0:T(8,128)(2,1)S(1)}, bf16[8,64,512]{2,1,0:T(8,128)(2,1)S(1)}, u32[]{:S(2)}, u32[]{:S(2)}) collective-permute-start(bf16[8,64,512]{2,1,0:T(8,128)(2,1)S(1)} %get-tuple-element.201.refs_0_), channel_id=1, source_target_pairs={{0,64},{16,80},{32,96},{48,112},{64,0},{80,16},{96,32},{112,48},{1... | collective-permute-start | bytes 1572872 | tf_op jit(solution)/shard_map/ppermute | solution.py:340
  42.5 4.3 %collective-permute-start.4 = (bf16[8,64,512]{2,1,0:T(8,128)(2,1)S(1)}, bf16[8,64,512]{2,1,0:T(8,128)(2,1)S(1)}, u32[]{:S(2)}, u32[]{:S(2)}) collective-permute-start(bf16[8,64,512]{2,1,0:T(8,128)(2,1)S(1)} %get-tuple-element.201.refs_0_), channel_id=1, source_target_pairs={{0,48},{16,32},{32,16},{48,0},{64,112},{80,96},{96,80},{112,64},{1... | collective-permute-start | bytes 1572872 | tf_op jit(solution)/shard_map/ppermute | solution.py:340
  46.9 0.0 collective-permute-done.2.refs_3_
  46.9 1.9 %collective-permute-start.3 = (bf16[8,64,512]{2,1,0:T(8,128)(2,1)S(1)}, bf16[8,64,512]{2,1,0:T(8,128)(2,1)S(1)}, u32[]{:S(2)}, u32[]{:S(2)}) collective-permute-start(bf16[8,64,512]{2,1,0:T(8,128)(2,1)S(1)} %get-tuple-element.201.refs_0_), channel_id=1, source_target_pairs={{0,16},{16,0},{32,48},{48,32},{64,80},{80,64},{96,112},{112,96},{1... | collective-permute-start | bytes 1572872 | tf_op jit(solution)/shard_map/ppermute | solution.py:340
  48.8 0.0 collective-permute-done.1.refs_2_
  48.9 0.0 collective-permute-done.refs_1_
  48.9 0.6 all-to-all-done.2.rows_ref
  49.5 0.0 copy-start
  49.5 3.2 %shrink_part.2 = (bf16[16,32,128]{2,1,0:T(8,128)(2,1)}, bf16[128,128]{1,0:T(8,128)(2,1)S(1)}, f32[64,128]{1,0:T(8,128)S(1)}) custom-call(bf16[8,16,640]{2,1,0:T(8,128)(2,1)S(1)} %all-to-all-done.2.rows_ref, bf16[8,64,512]{2,1,0:T(8,128)(2,1)S(1)} %get-tuple-element.197.refs_0_, bf16[8,64,512]{2,1,0:T(8,128)(2,1)} %collective-permute-done.refs_1_, ...), custom_call_target="tpu_custom_call" | custom-call | tf_op jit(solution)/shard_map/shrink_part/pallas_call | solution.py:395
  52.7 0.0 copy-done
  52.7 3.8 %all-to-all-start.3 = ((bf16[16,32,128]{2,1,0:T(8,128)(2,1)}), bf16[16,32,128]{2,1,0:T(8,128)(2,1)S(1)}, u32[]{:S(2)}, u32[]{:S(2)}) async-start(bf16[16,32,128]{2,1,0:T(8,128)(2,1)} %get-tuple-element.79), calls=%async_computation.3 | async-start | bytes 262144 | tf_op jit(solution)/shard_map/all_to_all | solution.py:411
  56.5 0.7 convert_convert_fusion
  57.2 0.1 copy.15
  57.3 0.8 convert_reduce_fusion
  60.4 0.0 collective-permute-done.5.refs_3_
  60.5 0.0 collective-permute-done.4.refs_2_
  60.5 1.3 %collective-permute-done.3.refs_1_ = bf16[8,64,512]{2,1,0:T(8,128)(2,1)S(1)} collective-permute-done((bf16[8,64,512]{2,1,0:T(8,128)(2,1)S(1)}, bf16[8,64,512]{2,1,0:T(8,128)(2,1)S(1)}, u32[]{:S(2)}, u32[]{:S(2)}) %collective-permute-start.3) | collective-permute-done | bytes 524320 | tf_op jit(solution)/shard_map/ppermute | solution.py:340
  61.7 4.0 %all-to-all-done.3.part_ref = bf16[16,32,128]{2,1,0:T(8,128)(2,1)S(1)} async-done(((bf16[16,32,128]{2,1,0:T(8,128)(2,1)}), bf16[16,32,128]{2,1,0:T(8,128)(2,1)S(1)}, u32[]{:S(2)}, u32[]{:S(2)}) %all-to-all-start.3) | async-done | bytes 131104 | tf_op jit(solution)/shard_map/all_to_all | solution.py:411
  65.7 0.7 expand_rows.2
  66.4 15.5 %all_to_all.26.part_ref = bf16[8,16,512]{2,1,0:T(8,128)(2,1)S(1)} all-to-all(bf16[8,16,512]{2,1,0:T(8,128)(2,1)S(1)} %get-tuple-element.82), channel_id=1, replica_groups={{0,96,128,224,256,352,384,480},{16,112,144,240,272,368,400,496},{32,64,..., dimensions={0} | all-to-all | bytes 262144 | tf_op jit(solution)/shard_map/all_to_all | solution.py:432
  82.0 0.6 returned_rows.1
  (1 shorter events, 0.0 us)
Async XLA Ops:
  0.6 12.9 %copy-start.1 = (bf16[8,2,64,512]{3,2,1,0:T(8,128)(2,1)S(1)}, bf16[8,2,64,512]{3,2,1,0:T(8,128)(2,1)}, u32[]{:S(2)}) copy-start(bf16[8,2,64,512]{3,2,1,0:T(8,128)(2,1)} %param.14) | copy-start | bytes 3145732
  3.3 23.3 %all-to-all-start.1 = ((bf16[16,16,640]{2,1,0:T(8,128)(2,1)}), bf16[16,16,640]{2,1,0:T(8,128)(2,1)S(1)}, u32[]{:S(2)}, u32[]{:S(2)}) async-start(bf16[16,16,640]{2,1,0:T(8,128)(2,1)} %get-tuple-element.76), calls=%async_computation.1 | async-start | bytes 655360 | tf_op jit(solution)/shard_map/all_to_all | solution.py:370
  13.6 33.3 %collective-permute-start.2 = (bf16[8,64,512]{2,1,0:T(8,128)(2,1)S(1)}, bf16[8,64,512]{2,1,0:T(8,128)(2,1)S(1)}, u32[]{:S(2)}, u32[]{:S(2)}) collective-permute-start(bf16[8,64,512]{2,1,0:T(8,128)(2,1)S(1)} %get-tuple-element.197.refs_0_), channel_id=1, source_target_pairs={{0,64},{16,80},{32,96},{48,112},{64,0},{80,16},{96,32},{112,48},{1... | collective-permute-start | bytes 1572872 | tf_op jit(solution)/shard_map/ppermute | solution.py:340
  16.1 32.8 %collective-permute-start.1 = (bf16[8,64,512]{2,1,0:T(8,128)(2,1)S(1)}, bf16[8,64,512]{2,1,0:T(8,128)(2,1)}, u32[]{:S(2)}, u32[]{:S(2)}) collective-permute-start(bf16[8,64,512]{2,1,0:T(8,128)(2,1)S(1)} %get-tuple-element.197.refs_0_), channel_id=1, source_target_pairs={{0,48},{16,32},{32,16},{48,0},{64,112},{80,96},{96,80},{112,64},{1... | collective-permute-start | bytes 1572872 | tf_op jit(solution)/shard_map/ppermute | solution.py:340
  20.5 28.4 %collective-permute-start = (bf16[8,64,512]{2,1,0:T(8,128)(2,1)S(1)}, bf16[8,64,512]{2,1,0:T(8,128)(2,1)}, u32[]{:S(2)}, u32[]{:S(2)}) collective-permute-start(bf16[8,64,512]{2,1,0:T(8,128)(2,1)S(1)} %get-tuple-element.197.refs_0_), channel_id=1, source_target_pairs={{0,16},{16,0},{32,48},{48,32},{64,80},{80,64},{96,112},{112,96},{1... | collective-permute-start | bytes 1572872 | tf_op jit(solution)/shard_map/ppermute | solution.py:340
  28.2 21.3 %all-to-all-start.2 = ((bf16[8,16,640]{2,1,0:T(8,128)(2,1)}), bf16[8,16,640]{2,1,0:T(8,128)(2,1)S(1)}, u32[]{:S(2)}, u32[]{:S(2)}) async-start(bf16[8,16,640]{2,1,0:T(8,128)(2,1)} %get-tuple-element.78), calls=%async_computation.2 | async-start | bytes 327680 | tf_op jit(solution)/shard_map/all_to_all | solution.py:387
  39.2 21.3 %collective-permute-start.5 = (bf16[8,64,512]{2,1,0:T(8,128)(2,1)S(1)}, bf16[8,64,512]{2,1,0:T(8,128)(2,1)S(1)}, u32[]{:S(2)}, u32[]{:S(2)}) collective-permute-start(bf16[8,64,512]{2,1,0:T(8,128)(2,1)S(1)} %get-tuple-element.201.refs_0_), channel_id=1, source_target_pairs={{0,64},{16,80},{32,96},{48,112},{64,0},{80,16},{96,32},{112,48},{1... | collective-permute-start | bytes 1572872 | tf_op jit(solution)/shard_map/ppermute | solution.py:340
  42.5 17.9 %collective-permute-start.4 = (bf16[8,64,512]{2,1,0:T(8,128)(2,1)S(1)}, bf16[8,64,512]{2,1,0:T(8,128)(2,1)S(1)}, u32[]{:S(2)}, u32[]{:S(2)}) collective-permute-start(bf16[8,64,512]{2,1,0:T(8,128)(2,1)S(1)} %get-tuple-element.201.refs_0_), channel_id=1, source_target_pairs={{0,48},{16,32},{32,16},{48,0},{64,112},{80,96},{96,80},{112,64},{1... | collective-permute-start | bytes 1572872 | tf_op jit(solution)/shard_map/ppermute | solution.py:340
  46.9 14.8 %collective-permute-start.3 = (bf16[8,64,512]{2,1,0:T(8,128)(2,1)S(1)}, bf16[8,64,512]{2,1,0:T(8,128)(2,1)S(1)}, u32[]{:S(2)}, u32[]{:S(2)}) collective-permute-start(bf16[8,64,512]{2,1,0:T(8,128)(2,1)S(1)} %get-tuple-element.201.refs_0_), channel_id=1, source_target_pairs={{0,16},{16,0},{32,48},{48,32},{64,80},{80,64},{96,112},{112,96},{1... | collective-permute-start | bytes 1572872 | tf_op jit(solution)/shard_map/ppermute | solution.py:340
  49.5 3.2 %copy-start = (bf16[8,16,640]{2,1,0:T(8,128)(2,1)}, bf16[8,16,640]{2,1,0:T(8,128)(2,1)S(1)}, u32[]{:S(2)}) copy-start(bf16[8,16,640]{2,1,0:T(8,128)(2,1)S(1)} %all-to-all-done.2.rows_ref) | copy-start | bytes 491524
  52.7 13.0 %all-to-all-start.3 = ((bf16[16,32,128]{2,1,0:T(8,128)(2,1)}), bf16[16,32,128]{2,1,0:T(8,128)(2,1)S(1)}, u32[]{:S(2)}, u32[]{:S(2)}) async-start(bf16[16,32,128]{2,1,0:T(8,128)(2,1)} %get-tuple-element.79), calls=%async_computation.3 | async-start | bytes 262144 | tf_op jit(solution)/shard_map/all_to_all | solution.py:411
